TPU v7x, 128 devices: a whole 4x4x4 slice. The times are simulated.
128 devices in a mesh: loop: 16 (over x_lo, z, core), group: 8 (over y, x_hi).
Axes of the slice: x: 4 (x_hi: 2, x_lo: 2; x = x_hi * 2 + x_lo), y: 4, z: 4, core: 2. Of those that a mesh axis runs over, the one named last changes fastest.
Arguments:
- projections: float32 [32768, 256], P(('loop', 'group')), may hold values from -3 to 3
- partners: int32 [32768], P(('loop', 'group')), may hold values from 0 to 32767, as said below
Outputs:
- view_loss: float32 [32768], P(('loop', 'group'))
- gradient: float32 [32768, 256], P(('loop', 'group'))
Inputs may be any that keep to these rules, and one draw needn't show every extreme that they name: partners[partners[i]] == i and partners[i] != i for every view: the views form 32768 / 2 disjoint pairs.
All inputs are finite; a program needn't handle non-finite values.
Results may differ from a plain program's by a relative error of at most 0.005.
Values may be sent and summed in bfloat16 or wider, within the bound.
A program may use at most 128 MiB of HBM per device.

v0:
```python
import jax
import jax.numpy as jnp
from jax import lax
from jax.sharding import PartitionSpec as P

epsilon = 1e-06
inverse_temp = 10.0
score_bound = 10.0


def tile_terms(row_low, partner_ids, row_index, col_block):
    logits = (
        lax.dot_general(
            row_low, col_block, (((1,), (1,)), ((), ())), preferred_element_type=jnp.float32
        )
        * inverse_temp
    )
    col_index = jnp.arange(col_block.shape[0], dtype=jnp.int32)
    tile_exp = jnp.where(
        col_index[None, :] == row_index[:, None], jnp.float32(0.0), jnp.exp(logits - score_bound)
    )
    paired = col_index[None, :] == partner_ids[:, None]
    return (logits, tile_exp, paired)


def tile_weights(tile_exp, paired, recip_rows, recip_cols):
    weights = tile_exp * (recip_rows[:, None] + recip_cols[None, :]) - 2.0 * paired.astype(
        jnp.float32
    )
    return weights.astype(jnp.bfloat16)


def on_device(projections, partners):
    inv_norm = lax.rsqrt(jnp.sum(projections * projections, axis=1) + epsilon)
    unit_rows = projections * inv_norm[:, None]
    row_low = unit_rows.astype(jnp.bfloat16)
    view_rows = row_low.shape[0]
    group_size = lax.axis_size("group")
    loop_index = lax.axis_index("loop")
    first_row = (loop_index * group_size + lax.axis_index("group")) * view_rows
    row_index = first_row + jnp.arange(view_rows, dtype=jnp.int32)
    group_block = lax.all_gather(row_low, "group", axis=0, tiled=True)
    logits, tile_exp, paired = tile_terms(
        row_low, partners, row_index, lax.all_gather(group_block, "loop", axis=0, tiled=True)
    )
    row_sums = jnp.sum(tile_exp, axis=1)
    positive = jnp.sum(jnp.where(paired, logits, jnp.float32(0.0)), axis=1)
    recip_own = 1.0 / row_sums
    recip_all = lax.all_gather(recip_own, ("loop", "group"), axis=0, tiled=True)
    shard_block = lax.all_gather(group_block, "loop", axis=0, tiled=True)
    logits, tile_exp, paired = tile_terms(row_low, partners, row_index, shard_block)
    weights = tile_weights(tile_exp, paired, recip_own, recip_all)
    grad_sum = jnp.dot(weights, shard_block, preferred_element_type=jnp.float32)
    view_loss = jnp.log(row_sums) + score_bound - positive
    grad_unit = grad_sum * inverse_temp
    along = jnp.sum(unit_rows * grad_unit, axis=1, keepdims=True)
    gradient = inv_norm[:, None] * (grad_unit - unit_rows * along)
    return (view_loss, gradient)


def solution(mesh):
    return jax.shard_map(
        on_device,
        mesh=mesh,
        in_specs=(P(("loop", "group"), None), P(("loop", "group"))),
        out_specs=(P(("loop", "group")), P(("loop", "group"), None)),
        check_vma=False,
    )
```

profile of v0, /device:TPU:0, one launch (start us, length us, event | category | flops | bytes accessed | tf_op | source)
XLA Modules:
  0.0 519.4 jit_solution(11519647565721614341)
XLA Ops:
  7.2 0.0 all-gather.4.cloned.1.call-start
  7.2 1.1 multiply_reduce_fusion.1
  8.3 1.1 copy.6
  9.4 0.7 multiply_convert_fusion
  10.0 0.0 all-gather.4.cloned.1.call-update
  10.1 0.0 all-gather.6.cloned.1.call-start
  10.1 48.3 %all-gather.4.cloned.1.call-done = bf16[2048,256]{0,1:T(8,128)(2,1)} async-done(((bf16[256,256]{0,1:T(8,128)(2,1)}), bf16[2048,256]{0,1:T(8,128)(2,1)}) %all-gather.4.cloned.1.call-update) | async-done | bytes 1048592 | tf_op jit(solution)/shard_map/all_gather | solution.py:42
  58.4 0.0 all-gather.6.cloned.1.call-update
  58.5 0.0 copy-start
  58.5 91.6 %all-gather.6.cloned.1.call-done = bf16[32768,256]{0,1:T(8,128)(2,1)} async-done(((bf16[2048,256]{0,1:T(8,128)(2,1)}), bf16[32768,256]{0,1:T(8,128)(2,1)}) %all-gather.6.cloned.1.call-update) | async-done | bytes 16777232 | tf_op jit(solution)/shard_map/all_gather | solution.py:44
  150.0 22.9 %fusion = (f32[256]{0:T(256)S(1)}, f32[256]{0:T(256)S(1)}, f32[256,32768]{1,0:T(8,128)}) fusion(s32[256]{0:T(256)S(1)} %iota_add_fusion, s32[256]{0:T(256)} %param.3, bf16[256,256]{0,1:T(8,128)(2,1)} %multiply_convert_fusion, bf16[32768,256]{0,1:T(8,128)(2,1)} %all-gather.6.cloned.1.call-done), kind=kOutput, calls=%fused_computation.6 | convolution fusion | flops 4362076160 | bytes 50466816 | tf_op jit(solution)/shard_map/dot_general | solution.py:13
  172.9 0.6 broadcast_divide_fusion
  173.5 316.5 %all-gather = f32[128,1,256]{2,1,0:T(1,128)S(1)} all-gather(f32[1,1,256]{2,1,0:T(1,128)S(1)} %bitcast.6), channel_id=1, replica_groups=mesh['loop'=16,'group'=8] {'loop','group'}, dimensions={0}, use_global_device_ids=true | all-gather | bytes 132096 | tf_op jit(solution)/shard_map/all_gather | solution.py:49
  490.0 0.0 copy-done
  490.0 21.7 %multiply_reduce_fusion = (f32[256]{0:T(256)S(1)}, f32[256,256]{0,1:T(8,128)S(1)}) fusion(f32[256,256]{0,1:T(8,128)S(1)} %copy.6, f32[256]{0:T(256)S(1)} %add_rsqrt_fusion, bf16[32768,256]{0,1:T(8,128)(2,1)} %all-gather.6.cloned.1.call-done, f32[256,32768]{1,0:T(8,128)} %get-tuple-element.10, f32[32768]{0:T(1024)S(1)} %bitcast.5, ...), kind=kOutput, calls=%fused_computation.10 | convolution fusion | flops 4370726912 | bytes 50992128 | tf_op jit(solution)/shard_map/dot_general | solution.py:53
  511.7 0.1 subtract_multiply_fusion
  511.7 0.8 copy.7
  (2 shorter events, 0.0 us)
Async XLA Ops:
  7.2 51.3 %all-gather.4.cloned.1.call-start = ((), (), s32[]{:S(2)}) async-start(), calls=%async_computation | async-start | bytes 1179648 | tf_op jit(solution)/shard_map/all_gather | solution.py:42
  10.1 140.0 %all-gather.6.cloned.1.call-start = ((), (), s32[]{:S(2)}) async-start(), calls=%async_computation.1 | async-start | bytes 17825792 | tf_op jit(solution)/shard_map/all_gather | solution.py:44
  58.5 431.5 %copy-start = (s32[256]{0:T(256)S(1)}, s32[256]{0:T(256)}, u32[]{:S(2)}) copy-start(s32[256]{0:T(256)} %param.3) | copy-start | bytes 3076
Sparse Core Ops, SparseCore 0:
  10.8 47.6 all-gather.3
  60.1 89.9 all-gather.5
where the time goes:
time: 520 us; the launch traced here: 519 us
  blocking collectives  317 us (61%)
  waiting for transfers between devices  140 us (27%)
  matrix products  44.5 us (9%)
  between operations  14.1 us (3%)
    all_gather x1, blocking collectives, on_device(): recip_all = lax.all_gather(recip_own, ('loop', 'group'), axis=0, tiled=True)  317 us
    all_gather x1, waiting for transfers between devices, on_device(): lax.all_gather(group_block, 'loop', axis=0, tiled=True)  91.6 us
    all_gather x1, waiting for transfers between devices, on_device(): group_block = lax.all_gather(row_low, 'group', axis=0, tiled=True)  48.3 us
    dot_general x1, matrix products, tile_terms(): lax.dot_general(row_low, col_block, (((1,), (1,)), ((), ())), preferred_e...  22.9 us
    dot_general x1, matrix products, on_device(): grad_sum = jnp.dot(weights, shard_block, preferred_element_type=jnp.float32)  21.7 us
  transfers between devices with their start and end apart: 2, of which 2 were waited for; matrix products, arithmetic and copies ran while one was open for 0% of the time, Pallas kernels for 0%

commit v1 on v0

v1 whole, which is shorter than its diff:
```python
import jax
import jax.numpy as jnp
from jax import lax
from jax.experimental import pallas as pl
from jax.experimental.pallas import tpu as pltpu
from jax.sharding import PartitionSpec as P

MESH = pl.DeviceIdType.MESH
F32, BF16 = jnp.float32, jnp.bfloat16
epsilon = 1e-06
inverse_temp = 10.0
LOG2E = 1.4426950408889634

PROJ = 256
BLK = 256
RING = 4
PLANE = 2 * RING * RING
COLS = PLANE * BLK
ROWS = RING * BLK

ORDER = [
    (0, 0), (1, 0), (3, 0), (0, 1), (0, 3), (1, 1), (3, 1), (1, 3),
    (3, 3), (2, 0), (0, 2), (2, 1), (2, 3), (1, 2), (3, 2), (2, 2),
]
STEP = {d: s for s, d in enumerate(ORDER)}


def own_pos(s):
    return 0 if s == 0 else 2 * s - 1


def sib_pos(s):
    return 2 * s + 2 if s < 15 else 31


def forwards(d):
    dx, dz = d
    out = []
    if d == (0, 0):
        return [(0, 2, (1, 0), (1, 0)), (0, 2, (3, 0), (-1, 0)), (0, 2, (0, 1), (0, 1)), (0, 2, (0, 3), (0, -1))]
    for half in (0, 1):
        a, b = (dx, dz) if half == 0 else (dz, dx)

        def there(a, b):
            return (a, b) if half == 0 else (b, a)

        first = 1 if half == 0 else 3
        if b == 0:
            if a == first:
                out.append((half, 1, there(2, 0), there(1 if first == 1 else -1, 0)))
            out.append((half, 1, there(a, 1), there(0, 1)))
            out.append((half, 1, there(a, 3), there(0, -1)))
        else:
            turn = 1 if a in (0, 1) else 3
            if b == turn:
                out.append((half, 1, there(a, 2), there(0, 1 if turn == 1 else -1)))
    return out


LEAD = 5
COMM_BEFORE = [[] for _ in range(16)]
for _s in range(LEAD, 16):
    COMM_BEFORE[min(_s - LEAD, _s - 1)].append(_s)


def transposed_sum(v):
    parts = [jnp.sum(jnp.transpose(v[i * 128 : (i + 1) * 128, :]), axis=0, keepdims=True) for i in range(2)]
    return jnp.concatenate(parts, axis=1)


def kernel(
    proj_ref, part_ref, loss_ref, grad_ref,
    u, u32, rows, e, acc, inv, enc, enc_s, pick,
    rs_send, rs_recv, r_cols, r_rows, ri, pos_send, pos_recv, g_acc, g_own, g_send, g_recv,
    own_sem, sib_sem, row_sem, enc_sem, rs_sem, rcol_sem, rrow_sem, pos_sem, g_sem, send_sem, local_sem,
):
    loop, group = lax.axis_index("loop"), lax.axis_index("group")
    core, z, x_lo = lax.rem(loop, 2), lax.rem(loop // 2, 4), loop // 8
    y, x_hi = group // 2, lax.rem(group, 2)
    x = x_hi * 2 + x_lo

    def dev(dx=0, dz=0, dy=0, dc=0):
        xx, zz, yy = lax.rem(x + dx + 4, 4), lax.rem(z + dz + 4, 4), lax.rem(y + dy + 4, 4)
        cc = 1 - core if dc else core
        return ((lax.rem(xx, 2) * 4 + zz) * 2 + cc, yy * 2 + xx // 2)

    n_send = [0]
    sent = []

    def remote(src, dst, recv, to):
        index = n_send[0]
        n_send[0] += 1

        def make():
            return pltpu.make_async_remote_copy(
                src_ref=src, dst_ref=dst, send_sem=send_sem.at[index], recv_sem=recv, device_id=to, device_id_type=MESH
            )

        sent.append(make)
        return make

    plane = [(dx, dz, dc) for dc in (0, 1) for dx in range(4) for dz in range(4) if (dx, dz, dc) != (0, 0, 0)]
    barrier = pltpu.get_barrier_semaphore()
    for dx, dz, dc in plane:
        pl.semaphore_signal(barrier, inc=1, device_id=dev(dx, dz, 0, dc), device_id_type=MESH)
    for k in (1, 2, 3):
        pl.semaphore_signal(barrier, inc=1, device_id=dev(dy=k), device_id_type=MESH)

    proj = proj_ref[...]
    inv_norm = lax.rsqrt(jnp.sum(proj * proj, axis=1, keepdims=True) + epsilon)
    inv[...] = jnp.broadcast_to(inv_norm, inv.shape)
    low = (proj * inv_norm).astype(BF16)
    u[0] = low
    rows[0] = low

    p = part_ref[...]
    off, blk = p & 255, p >> 8
    p_group, p_loop = blk & 7, blk >> 3
    p_x = ((p_group & 1) << 1) + (p_loop >> 3)
    p_z, p_c = (p_loop >> 1) & 3, p_loop & 1
    key = (p_c ^ core) * 16 + ((x - p_x) & 3) * 4 + ((z - p_z) & 3)
    place = jnp.zeros_like(p)
    for dx in range(4):
        for dz in range(4):
            s = STEP[(dx, dz)]
            place = jnp.where(key == dx * 4 + dz, own_pos(s), place)
            place = jnp.where(key == 16 + dx * 4 + dz, sib_pos(s), place)
    enc[0] = (p_group >> 1) * COLS + place * BLK + off
    u32[COLS : COLS + 8, :] = jnp.zeros((8, PROJ), F32)
    acc[...] = jnp.zeros_like(acc)

    pl.semaphore_wait(barrier, len(plane) + 3)

    row_copies = []
    for k in (2, 1, 3):
        row_copies.append(remote(u.at[0], rows.at[k], row_sem.at[k - 1], dev(dy=k)))
    enc_copies = [remote(enc.at[0], enc.at[k], enc_sem.at[k - 1], dev(dy=k)) for k in (1, 2, 3)]

    def piece(pos, half, halves):
        return u.at[pos, pl.ds(half * 128, halves * 128), :]

    comm = []
    for s, d in enumerate(ORDER):
        out = []
        for half, halves, there, (ddx, ddz) in forwards(d):
            t = STEP[there]
            out.append(
                remote(piece(own_pos(s), half, halves), piece(own_pos(t), half, halves), own_sem.at[t, half], dev(ddx, ddz))
            )
        out.append(remote(u.at[own_pos(s)], u.at[sib_pos(s)], sib_sem.at[s], dev(dc=1)))
        comm.append(out)

    def wait_for(ref, sem):
        pltpu.make_async_copy(ref, ref, sem).wait()

    def comm_step(s):
        if s in (1, 2, 3, 4):
            wait_for(u.at[own_pos(s)], own_sem.at[s, 0])
        elif s > 0:
            for half in (0, 1):
                wait_for(piece(own_pos(s), half, 1), own_sem.at[s, half])
        for make in comm[s]:
            make().start()

    comm_step(0)
    for make in row_copies + enc_copies:
        make().start()
    for s in range(1, LEAD):
        comm_step(s)
    for k in (1, 2, 3):
        wait_for(rows.at[k], row_sem.at[k - 1])

    scale = inverse_temp * LOG2E
    r_iota = lax.broadcasted_iota(jnp.int32, (BLK, BLK), 0)
    c_iota = lax.broadcasted_iota(jnp.int32, (BLK, BLK), 1)

    def compute(i, carry):
        for t in range(16):
            if COMM_BEFORE[t]:

                @pl.when(i == t)
                def _():
                    for s in COMM_BEFORE[t]:
                        comm_step(s)

        @pl.when(i >= 1)
        def _():
            wait_for(u.at[2 * i], sib_sem.at[i - 1])

        @pl.when(i == 15)
        def _():
            wait_for(u.at[31], sib_sem.at[15])

        for b in (0, 1):
            pos = 2 * i + b
            block = u[pos]
            u32[pl.ds(pl.multiple_of(pos * BLK, BLK), BLK), :] = block.astype(F32)
            for k in range(RING):
                dots = lax.dot_general(rows[k], block, (((1,), (1,)), ((), ())), preferred_element_type=F32)
                ex = jnp.exp2(dots * scale)
                if k == 0 and b == 0:
                    ex = jnp.where(r_iota == c_iota + i * BLK, 0.0, ex)
                acc[k] += ex[:, :128] + ex[:, 128:]
                e[k, pos] = ex.astype(BF16)
        return carry

    lax.fori_loop(0, 16, compute, 0)

    for k in range(RING):
        rs_send[k] = transposed_sum(acc[k])
    rs_copies = [remote(rs_send.at[k], rs_recv.at[k], rs_sem.at[k - 1], dev(dy=-k)) for k in (2, 1, 3)]
    for make in rs_copies:
        make().start()
    for k in (1, 2, 3):
        wait_for(enc.at[k], enc_sem.at[k - 1])
    to_smem = pltpu.make_async_copy(enc, enc_s, local_sem)
    to_smem.start()
    to_smem.wait()
    for k in (1, 2, 3):
        wait_for(rs_recv.at[k], rs_sem.at[k - 1])
    row_sums = rs_send[0] + rs_recv[1] + rs_recv[2] + rs_recv[3]
    recip = 1.0 / row_sums
    r_cols[0] = recip
    r_rows[0] = recip
    r_copies = []
    for dx, dz, dc in plane:
        s = STEP[(dx, dz)]
        pos = sib_pos(s) if dc else own_pos(s)
        r_copies.append(remote(r_cols.at[0], r_cols.at[pos], rcol_sem.at[pos], dev(dx, dz, 0, dc)))
    for k in (1, 2, 3):
        r_copies.append(remote(r_cols.at[0], r_rows.at[k], rrow_sem.at[k - 1], dev(dy=k)))
    for make in r_copies:
        make().start()

    for k in range(RING):

        def fetch(j, carry):
            for t in range(8):
                i = j * 8 + t
                v = enc_s[k, 0, i]
                at = jnp.where(v // COLS == y, lax.rem(v, COLS), COLS)
                pick[k, pl.ds(i, 1), :] = u32[pl.ds(at, 1), :]
            return carry

        lax.fori_loop(0, BLK // 8, fetch, 0)
    for k in range(RING):
        q = rows[k].astype(F32) * pick[k]
        pos_send[k] = transposed_sum(q[:, :128] + q[:, 128:]) * inverse_temp
    pos_copies = [remote(pos_send.at[k], pos_recv.at[k], pos_sem.at[k - 1], dev(dy=-k)) for k in (1, 2, 3)]
    for make in pos_copies:
        make().start()

    for k in (1, 2, 3):
        wait_for(r_rows.at[k], rrow_sem.at[k - 1])
    for dx, dz, dc in plane:
        s = STEP[(dx, dz)]
        pos = sib_pos(s) if dc else own_pos(s)
        wait_for(r_cols.at[pos], rcol_sem.at[pos])
    for k in range(RING):
        r = r_rows[k]
        for h in (0, 1):
            part = jnp.broadcast_to(r[:, h * 128 : (h + 1) * 128], (128, 128))
            ri[k, h * 128 : (h + 1) * 128, :] = jnp.transpose(part)

    g_copies = {k: remote(g_send.at[k], g_recv.at[k], g_sem.at[k - 1], dev(dy=-k)) for k in (1, 2, 3)}
    for k in (2, 1, 3, 0):
        g_acc[...] = jnp.zeros_like(g_acc)

        def weigh(i, carry):
            total = g_acc[...]
            r_row = jnp.concatenate([ri[k], ri[k]], axis=1)
            for b in range(4):
                pos = 4 * i + b
                w = e[k, pos].astype(F32) * (r_row + r_cols[pos])
                total += jnp.dot(w.astype(BF16), u[pos], preferred_element_type=F32)
            g_acc[...] = total
            return carry

        lax.fori_loop(0, PLANE // 4, weigh, 0)
        g = inverse_temp * (g_acc[...] - 2.0 * pick[k])
        if k:
            g_send[k] = g.astype(BF16)
            g_copies[k]().start()
        else:
            g_own[...] = g

    for k in (1, 2, 3):
        wait_for(pos_recv.at[k], pos_sem.at[k - 1])
    positive = pos_send[0] + pos_recv[1] + pos_recv[2] + pos_recv[3]
    loss_ref[...] = jnp.log(row_sums) - positive
    for k in (1, 2, 3):
        wait_for(g_recv.at[k], g_sem.at[k - 1])
    grad_unit = g_own[...] + g_recv[1].astype(F32) + g_recv[2].astype(F32) + g_recv[3].astype(F32)
    inv_b = jnp.concatenate([inv[...], inv[...]], axis=1)
    unit = proj_ref[...] * inv_b
    along = jnp.sum(unit * grad_unit, axis=1, keepdims=True)
    grad_ref[...] = inv_b * (grad_unit - unit * along)

    for make in sent:
        make().wait_send()


N_SEND = 150


def on_device(projections, partners):
    dma = pltpu.SemaphoreType.DMA
    vmem = pl.BlockSpec(memory_space=pltpu.VMEM)
    loss, grad = pl.pallas_call(
        kernel,
        out_shape=(jax.ShapeDtypeStruct((1, BLK), F32), jax.ShapeDtypeStruct((BLK, PROJ), F32)),
        in_specs=[vmem, vmem],
        out_specs=(vmem, vmem),
        scratch_shapes=[
            pltpu.VMEM((PLANE, BLK, PROJ), BF16),
            pltpu.VMEM((COLS + 8, PROJ), F32),
            pltpu.VMEM((RING, BLK, PROJ), BF16),
            pltpu.VMEM((RING, PLANE, BLK, BLK), BF16),
            pltpu.VMEM((RING, BLK, 128), F32),
            pltpu.VMEM((BLK, 128), F32),
            pltpu.VMEM((RING, 1, BLK), jnp.int32),
            pltpu.SMEM((RING, 1, BLK), jnp.int32),
            pltpu.VMEM((RING, BLK, PROJ), F32),
            pltpu.VMEM((RING, 1, BLK), F32),
            pltpu.VMEM((RING, 1, BLK), F32),
            pltpu.VMEM((PLANE, 1, BLK), F32),
            pltpu.VMEM((RING, 1, BLK), F32),
            pltpu.VMEM((RING, BLK, 128), F32),
            pltpu.VMEM((RING, 1, BLK), F32),
            pltpu.VMEM((RING, 1, BLK), F32),
            pltpu.VMEM((BLK, PROJ), F32),
            pltpu.VMEM((BLK, PROJ), F32),
            pltpu.VMEM((RING, BLK, PROJ), BF16),
            pltpu.VMEM((RING, BLK, PROJ), BF16),
            dma((16, 2)), dma((16,)), dma((3,)), dma((3,)), dma((3,)), dma((PLANE,)), dma((3,)), dma((3,)), dma((3,)),
            dma((N_SEND,)), dma,
        ],
        compiler_params=pltpu.CompilerParams(
            collective_id=0, has_side_effects=True, vmem_limit_bytes=48 * 1024 * 1024
        ),
        cost_estimate=pl.CostEstimate(flops=4 * ROWS * COLS * PROJ, bytes_accessed=8 << 20, transcendentals=ROWS * COLS),
    )(projections, partners.reshape(1, BLK))
    return loss.reshape(BLK), grad


def solution(mesh):
    return jax.shard_map(
        on_device,
        mesh=mesh,
        in_specs=(P(("loop", "group"), None), P(("loop", "group"))),
        out_specs=(P(("loop", "group")), P(("loop", "group"), None)),
        check_vma=False,
    )
```

time: 520 us -> 66.5 us (0.13)
  blocking collectives: 317 us -> 0 us
  waiting for transfers between devices: 140 us -> 0 us
  Pallas kernels: 0 us -> 62.8 us
  matrix products: 44.5 us -> 0 us
  between operations: 14.1 us -> 0.65 us
    all_gather x1 -> x0, blocking collectives: 317 us -> none  [on_device(): recip_all = lax.all_gather(recip_own, ('loop', 'group'), axis=0, tiled=True)]
    all_gather x2 -> x0, waiting for transfers between devices: 140 us -> none  [the longest x1 91.6 us: on_device(): lax.all_gather(group_block, 'loop', axis=0, tiled=True)]
    pallas_call x0 -> x1, Pallas kernels: none -> 62.8 us  [on_device(): pl.pallas_call(kernel, out_shape=(jax.ShapeDtypeStruct((1, BLK), F32), ja...]
    dot_general x2 -> x0, matrix products: 44.5 us -> none  [the longest x1 22.9 us: tile_terms(): lax.dot_general(row_low, col_block, (((1,), (1,)), ((), ())), preferred_e...]
  transfers between devices with their start and end apart: 2 -> 0, of which waited for: 2 -> 0; matrix products, arithmetic and copies ran while one was open for 0% -> 0% of each run, Pallas kernels for 0% -> 0%
where the time goes in v1:
time: 66.5 us; the launch traced here: 66.3 us
  Pallas kernels  62.8 us (94%)
  local copies, waits for them, and re-layouts  2.89 us (4%)
    pallas_call x1, Pallas kernels, on_device(): pl.pallas_call(kernel, out_shape=(jax.ShapeDtypeStruct((1, BLK), F32), ja...  62.8 us
    unnamed x6, local copies, waits for them, and re-layouts  2.89 us

profile of v1, /device:TPU:0, one launch (start us, length us, event | category | flops | bytes accessed | tf_op | source)
XLA Modules:
  0.0 66.3 jit_solution(2947565148937697317)
XLA Ops:
  0.6 0.0 copy-start.1
  0.6 0.7 %copy-done.1 = s32[256]{0:T(256)S(1)} copy-done((s32[256]{0:T(256)S(1)}, s32[256]{0:T(256)}, u32[]{:S(2)}) %copy-start.1) | copy-done | bytes 1048
  1.3 0.0 copy-start
  1.3 0.9 %copy-done = f32[256,256]{1,0:T(8,128)S(1)} copy-done((f32[256,256]{1,0:T(8,128)S(1)}, f32[256,256]{1,0:T(8,128)}, u32[]{:S(2)}) %copy-start) | copy-done | bytes 262168
  2.3 62.8 %shard_map.41 = (f32[1,256]{1,0:T(1,128)S(1)}, f32[256,256]{1,0:T(8,128)S(1)}) custom-call(f32[256,256]{1,0:T(8,128)S(1)} %copy-done, s32[1,256]{1,0:T(1,128)S(1)} %bitcast.3), custom_call_target="tpu_custom_call" | custom-call | flops 8589934592 | bytes 8388608 | tf_op jit(solution)/shard_map/pallas_call | solution.py:309
  65.1 0.6 copy.6
  65.6 0.7 %copy.7 = f32[256,256]{1,0:T(8,128)} copy(f32[256,256]{1,0:T(8,128)S(1)} %get-tuple-element.9) | data formatting | bytes 524288
Async XLA Ops:
  0.6 0.7 %copy-start.1 = (s32[256]{0:T(256)S(1)}, s32[256]{0:T(256)}, u32[]{:S(2)}) copy-start(s32[256]{0:T(256)} %param.3) | copy-start | bytes 3076
  1.3 0.9 %copy-start = (f32[256,256]{1,0:T(8,128)S(1)}, f32[256,256]{1,0:T(8,128)}, u32[]{:S(2)}) copy-start(f32[256,256]{1,0:T(8,128)} %proj_ref.1) | copy-start | bytes 786436

commit v2 on v1

v2 whole, which is shorter than its diff:
```python
import jax
import jax.numpy as jnp
from jax import lax
from jax.experimental import pallas as pl
from jax.experimental.pallas import tpu as pltpu
from jax.sharding import PartitionSpec as P

MESH = pl.DeviceIdType.MESH
F32, BF16 = jnp.float32, jnp.bfloat16
epsilon = 1e-06
inverse_temp = 10.0
LOG2E = 1.4426950408889634

PROJ = 256
BLK = 256
RING = 4
PLANE = 2 * RING * RING
COLS = PLANE * BLK
ROWS = RING * BLK

ORDER = [
    (0, 0), (1, 0), (3, 0), (0, 1), (0, 3), (2, 0), (0, 2), (1, 1),
    (3, 1), (1, 3), (3, 3), (1, 2), (3, 2), (2, 1), (2, 3), (2, 2),
]
STEP = {d: s for s, d in enumerate(ORDER)}
DY = (2, 1, 3, 0)
SLOT = {dy: k for k, dy in enumerate(DY)}
OWN = SLOT[0]


def own_pos(s):
    return 0 if s == 0 else 2 * s - 1


def sib_pos(s):
    return 2 * s + 2 if s < 15 else 31


def transposed_sum(v):
    parts = [jnp.sum(jnp.transpose(v[i * 128 : (i + 1) * 128, :]), axis=0, keepdims=True) for i in range(2)]
    return jnp.concatenate(parts, axis=1)


def kernel(
    proj_hbm, part_hbm, loss_ref, grad_ref,
    proj_ref, part_ref, u, u32, rows, e, acc, inv, enc, enc_s, pick,
    rs_send, rs_recv, r_cols, r_rows, ri, pos_send, pos_recv, g_own, g_send, g_recv,
    own_sem, sib_sem, row_sem, enc_sem, rs_sem, rcol_sem, rrow_sem, pos_sem, g_sem, send_sem, local_sem, in_sem,
):
    loop, group = lax.axis_index("loop"), lax.axis_index("group")
    core, z, x_lo = lax.rem(loop, 2), lax.rem(loop // 2, 4), loop // 8
    y, x_hi = group // 2, lax.rem(group, 2)
    x = x_hi * 2 + x_lo

    def dev(dx=0, dz=0, dy=0, dc=0):
        xx, zz, yy = lax.rem(x + dx + 4, 4), lax.rem(z + dz + 4, 4), lax.rem(y + dy + 4, 4)
        cc = 1 - core if dc else core
        return ((lax.rem(xx, 2) * 4 + zz) * 2 + cc, yy * 2 + xx // 2)

    n_send = [0]
    sent = []

    def remote(src, dst, recv, to):
        index = n_send[0]
        n_send[0] += 1

        def make():
            return pltpu.make_async_remote_copy(
                src_ref=src, dst_ref=dst, send_sem=send_sem.at[index], recv_sem=recv, device_id=to, device_id_type=MESH
            )

        sent.append(make)
        return make

    proj_in = pltpu.make_async_copy(proj_hbm, proj_ref, in_sem.at[0])
    part_in = pltpu.make_async_copy(part_hbm, part_ref, in_sem.at[1])
    proj_in.start()
    part_in.start()
    plane = [(dx, dz, dc) for dc in (0, 1) for dz in (2, 1, 3, 0) for dx in (2, 1, 3, 0) if (dx, dz, dc) != (0, 0, 0)]
    near = [dev(dx=k) for k in (1, 2, 3)] + [dev(dz=k) for k in (1, 2, 3)] + [dev(dy=k) for k in (1, 2, 3)] + [dev(dc=1)]
    barrier = pltpu.get_barrier_semaphore()
    for to in near:
        pl.semaphore_signal(barrier, inc=1, device_id=to, device_id_type=MESH)

    proj_in.wait()
    proj = proj_ref[...]
    inv_norm = lax.rsqrt(jnp.sum(proj * proj, axis=1, keepdims=True) + epsilon)
    inv[...] = jnp.broadcast_to(inv_norm, inv.shape)
    low = (proj * inv_norm).astype(BF16)
    u[0] = low
    rows[OWN] = low
    part_in.wait()

    p = part_ref[...]
    off, blk = p & 255, p >> 8
    p_group, p_loop = blk & 7, blk >> 3
    p_x = ((p_group & 1) << 1) + (p_loop >> 3)
    p_z, p_c = (p_loop >> 1) & 3, p_loop & 1
    key = (p_c ^ core) * 16 + ((x - p_x) & 3) * 4 + ((z - p_z) & 3)
    place = jnp.zeros_like(p)
    for dx in range(4):
        for dz in range(4):
            s = STEP[(dx, dz)]
            place = jnp.where(key == dx * 4 + dz, own_pos(s), place)
            place = jnp.where(key == 16 + dx * 4 + dz, sib_pos(s), place)
    enc[OWN] = (p_group >> 1) * COLS + place * BLK + off
    u32[COLS : COLS + 8, :] = jnp.zeros((8, PROJ), F32)
    acc[...] = jnp.zeros_like(acc)

    pl.semaphore_wait(barrier, len(near))

    def wait_for(ref, sem):
        pltpu.make_async_copy(ref, ref, sem).wait()

    line = [(k, DY[k]) for k in range(RING) if DY[k]]
    row_copies = [remote(u.at[0], rows.at[k], row_sem.at[k], dev(dy=dy)) for k, dy in line]
    enc_copies = [remote(enc.at[OWN], enc.at[k], enc_sem.at[k], dev(dy=dy)) for k, dy in line]

    def piece(s, half):
        return u.at[own_pos(s), pl.ds(half * 128, 128), :]

    def along(half, d):
        return (d, 0) if half == 0 else (0, d)

    def push(s, half, axis, d):
        dx, dz = ORDER[s]
        t = STEP[((dx + d) % 4, dz) if axis == 0 else (dx, (dz + d) % 4)]
        remote(piece(s, half), piece(t, half), own_sem.at[t, half], dev(dx=d) if axis == 0 else dev(dz=d))().start()

    def wait_half(s, half):
        wait_for(piece(s, half), own_sem.at[s, half])

    sib_copies = [remote(u.at[own_pos(s)], u.at[sib_pos(s)], sib_sem.at[s], dev(dc=1)) for s in range(16)]

    for half in (0, 1):
        for d in (1, 3, 2):
            push(0, half, half, d)
    for k in (1, 2, 0):
        row_copies[k]().start()
    for half in (0, 1):
        for d in (1, 3, 2):
            push(0, half, 1 - half, d)
    sib_copies[0]().start()
    for make in enc_copies:
        make().start()
    for d in (1, 3, 2):
        for half in (0, 1):
            s = STEP[along(half, d)]
            wait_half(s, half)
            for f in (1, 3, 2):
                push(s, half, 1 - half, f)
    for s in range(1, 7):
        wait_half(s, 0 if ORDER[s][0] == 0 else 1)
        sib_copies[s]().start()
    for k, dy in line:
        wait_for(rows.at[k], row_sem.at[k])

    def comm_step(s):
        wait_half(s, 0)
        wait_half(s, 1)
        sib_copies[s]().start()

    scale = inverse_temp * LOG2E
    r_iota = lax.broadcasted_iota(jnp.int32, (BLK, BLK), 0)
    c_iota = lax.broadcasted_iota(jnp.int32, (BLK, BLK), 1)

    def compute(i, carry):
        for t in range(16):
            if 7 <= t + 1 <= 15:

                @pl.when(i == t)
                def _():
                    comm_step(t + 1)

        @pl.when(i >= 1)
        def _():
            wait_for(u.at[2 * i], sib_sem.at[i - 1])

        @pl.when(i == 15)
        def _():
            wait_for(u.at[31], sib_sem.at[15])

        for b in (0, 1):
            pos = 2 * i + b
            block = u[pos]
            u32[pl.ds(pl.multiple_of(pos * BLK, BLK), BLK), :] = block.astype(F32)
            for k in range(RING):
                dots = lax.dot_general(rows[k], block, (((1,), (1,)), ((), ())), preferred_element_type=F32)
                ex = jnp.exp2(dots * scale)
                if k == OWN and b == 0:
                    ex = jnp.where(r_iota == c_iota + i * BLK, 0.0, ex)
                acc[k] += ex[:, :128] + ex[:, 128:]
                e[k, pos] = ex.astype(BF16)
        return carry

    lax.fori_loop(0, 16, compute, 0)

    for k in range(RING):
        rs_send[k] = transposed_sum(acc[k])
    rs_copies = [remote(rs_send.at[k], rs_recv.at[k], rs_sem.at[k], dev(dy=-dy)) for k, dy in line]
    for make in rs_copies:
        make().start()
    for k, dy in line:
        wait_for(enc.at[k], enc_sem.at[k])
    to_smem = pltpu.make_async_copy(enc, enc_s, local_sem)
    to_smem.start()
    to_smem.wait()
    for k, dy in line:
        wait_for(rs_recv.at[k], rs_sem.at[k])
    row_sums = rs_send[OWN] + rs_recv[0] + rs_recv[1] + rs_recv[2]
    recip = 1.0 / row_sums
    r_cols[0] = recip
    r_rows[OWN] = recip
    r_copies = []
    for dx, dz, dc in plane:
        s = STEP[(dx, dz)]
        pos = sib_pos(s) if dc else own_pos(s)
        r_copies.append(remote(r_cols.at[0], r_cols.at[pos], rcol_sem.at[pos], dev(dx, dz, 0, dc)))
    for k, dy in line:
        r_copies.append(remote(r_cols.at[0], r_rows.at[k], rrow_sem.at[k], dev(dy=dy)))
    for make in r_copies:
        make().start()

    for k in range(RING):

        def fetch(j, carry):
            for t in range(8):
                i = j * 8 + t
                v = enc_s[k, 0, i]
                at = jnp.where(v // COLS == y, lax.rem(v, COLS), COLS)
                pick[k, pl.ds(i, 1), :] = u32[pl.ds(at, 1), :]
            return carry

        lax.fori_loop(0, BLK // 8, fetch, 0)
    for k in range(RING):
        q = rows[k].astype(F32) * pick[k]
        pos_send[k] = transposed_sum(q[:, :128] + q[:, 128:]) * inverse_temp
    pos_copies = [remote(pos_send.at[k], pos_recv.at[k], pos_sem.at[k], dev(dy=-dy)) for k, dy in line]
    for make in pos_copies:
        make().start()

    for k, dy in line:
        wait_for(r_rows.at[k], rrow_sem.at[k])
    for dx, dz, dc in plane:
        s = STEP[(dx, dz)]
        pos = sib_pos(s) if dc else own_pos(s)
        wait_for(r_cols.at[pos], rcol_sem.at[pos])
    for k in range(RING):
        r = r_rows[k]
        for h in (0, 1):
            part = jnp.broadcast_to(r[:, h * 128 : (h + 1) * 128], (128, 128))
            ri[k, h * 128 : (h + 1) * 128, :] = jnp.transpose(part)

    g_copies = [remote(g_send.at[k], g_recv.at[k], g_sem.at[k], dev(dy=-dy)) for k, dy in line]

    def weigh(k, carry):
        r_row = jnp.concatenate([ri[k], ri[k]], axis=1)
        total = jnp.zeros((BLK, PROJ), F32)
        for pos in range(PLANE):
            w = e[k, pos].astype(F32) * (r_row + r_cols[pos])
            total += jnp.dot(w.astype(BF16), u[pos], preferred_element_type=F32)
        g = inverse_temp * (total - 2.0 * pick[k])
        g_own[...] = g
        g_send[k] = g.astype(BF16)
        for t in range(3):

            @pl.when(k == t)
            def _():
                g_copies[t]().start()

        return carry

    lax.fori_loop(0, RING, weigh, 0)

    for k, dy in line:
        wait_for(pos_recv.at[k], pos_sem.at[k])
    positive = pos_send[OWN] + pos_recv[0] + pos_recv[1] + pos_recv[2]
    loss_ref[...] = jnp.log(row_sums) - positive
    for k, dy in line:
        wait_for(g_recv.at[k], g_sem.at[k])
    grad_unit = g_own[...] + g_recv[0].astype(F32) + g_recv[1].astype(F32) + g_recv[2].astype(F32)
    inv_b = jnp.concatenate([inv[...], inv[...]], axis=1)
    unit = proj_ref[...] * inv_b
    along = jnp.sum(unit * grad_unit, axis=1, keepdims=True)
    grad_ref[...] = inv_b * (grad_unit - unit * along)

    for make in sent:
        make().wait_send()


N_SEND = 150


def on_device(projections, partners):
    dma = pltpu.SemaphoreType.DMA
    vmem = pl.BlockSpec(memory_space=pltpu.VMEM)
    loss, grad = pl.pallas_call(
        kernel,
        out_shape=(jax.ShapeDtypeStruct((1, BLK), F32), jax.ShapeDtypeStruct((BLK, PROJ), F32)),
        in_specs=[pl.BlockSpec(memory_space=pltpu.HBM)] * 2,
        out_specs=(vmem, vmem),
        scratch_shapes=[
            pltpu.VMEM((BLK, PROJ), F32),
            pltpu.VMEM((1, BLK), jnp.int32),
            pltpu.VMEM((PLANE, BLK, PROJ), BF16),
            pltpu.VMEM((COLS + 8, PROJ), F32),
            pltpu.VMEM((RING, BLK, PROJ), BF16),
            pltpu.VMEM((RING, PLANE, BLK, BLK), BF16),
            pltpu.VMEM((RING, BLK, 128), F32),
            pltpu.VMEM((BLK, 128), F32),
            pltpu.VMEM((RING, 1, BLK), jnp.int32),
            pltpu.SMEM((RING, 1, BLK), jnp.int32),
            pltpu.VMEM((RING, BLK, PROJ), F32),
            pltpu.VMEM((RING, 1, BLK), F32),
            pltpu.VMEM((RING, 1, BLK), F32),
            pltpu.VMEM((PLANE, 1, BLK), F32),
            pltpu.VMEM((RING, 1, BLK), F32),
            pltpu.VMEM((RING, BLK, 128), F32),
            pltpu.VMEM((RING, 1, BLK), F32),
            pltpu.VMEM((RING, 1, BLK), F32),
            pltpu.VMEM((BLK, PROJ), F32),
            pltpu.VMEM((RING, BLK, PROJ), BF16),
            pltpu.VMEM((RING, BLK, PROJ), BF16),
            dma((16, 2)), dma((16,)), dma((3,)), dma((3,)), dma((3,)), dma((PLANE,)), dma((3,)), dma((3,)), dma((3,)),
            dma((N_SEND,)), dma, dma((2,)),
        ],
        compiler_params=pltpu.CompilerParams(
            collective_id=0, has_side_effects=True, vmem_limit_bytes=48 * 1024 * 1024
        ),
        cost_estimate=pl.CostEstimate(flops=4 * ROWS * COLS * PROJ, bytes_accessed=8 << 20, transcendentals=ROWS * COLS),
    )(projections, partners.reshape(1, BLK))
    return loss.reshape(BLK), grad


def solution(mesh):
    return jax.shard_map(
        on_device,
        mesh=mesh,
        in_specs=(P(("loop", "group"), None), P(("loop", "group"))),
        out_specs=(P(("loop", "group")), P(("loop", "group"), None)),
        check_vma=False,
    )
```

time: 66.5 us -> 56.5 us (0.85)
  Pallas kernels: 62.8 us -> 52.6 us
    pallas_call x1, Pallas kernels: 62.8 us -> 52.6 us  [on_device(): pl.pallas_call(kernel, out_shape=(jax.ShapeDtypeStruct((1, BLK), F32), ja...]
where the time goes in v2:
time: 56.5 us; the launch traced here: 56.1 us
  Pallas kernels  52.6 us (93%)
  local copies, waits for them, and re-layouts  2.89 us (5%)
  between operations  0.65 us (1%)
    pallas_call x1, Pallas kernels, on_device(): pl.pallas_call(kernel, out_shape=(jax.ShapeDtypeStruct((1, BLK), F32), ja...  52.6 us
    unnamed x6, local copies, waits for them, and re-layouts  2.89 us

profile of v2, /device:TPU:0, one launch (start us, length us, event | category | flops | bytes accessed | tf_op | source)
XLA Modules:
  0.0 56.1 jit_solution(11746428055500682540)
XLA Ops:
  0.6 0.0 copy-start.1
  0.6 0.7 %copy-done.1 = s32[256]{0:T(256)S(1)} copy-done((s32[256]{0:T(256)S(1)}, s32[256]{0:T(256)}, u32[]{:S(2)}) %copy-start.1) | copy-done | bytes 1048
  1.3 0.0 copy-start
  1.3 0.9 %copy-done = f32[256,256]{1,0:T(8,128)S(1)} copy-done((f32[256,256]{1,0:T(8,128)S(1)}, f32[256,256]{1,0:T(8,128)}, u32[]{:S(2)}) %copy-start) | copy-done | bytes 262168
  2.3 52.6 %shard_map.41 = (f32[1,256]{1,0:T(1,128)S(1)}, f32[256,256]{1,0:T(8,128)S(1)}) custom-call(f32[256,256]{1,0:T(8,128)S(1)} %copy-done, s32[1,256]{1,0:T(1,128)S(1)} %bitcast.3), custom_call_target="tpu_custom_call" | custom-call | flops 8589934592 | bytes 8388608 | tf_op jit(solution)/shard_map/pallas_call | solution.py:297
  54.8 0.6 %copy.6 = f32[256]{0:T(256)} copy(f32[256]{0:T(256)S(1)} %bitcast.2) | data formatting | bytes 2048
  55.4 0.7 %copy.7 = f32[256,256]{1,0:T(8,128)} copy(f32[256,256]{1,0:T(8,128)S(1)} %get-tuple-element.9) | data formatting | bytes 524288
Async XLA Ops:
  0.6 0.7 %copy-start.1 = (s32[256]{0:T(256)S(1)}, s32[256]{0:T(256)}, u32[]{:S(2)}) copy-start(s32[256]{0:T(256)} %param.3) | copy-start | bytes 3076
  1.3 0.9 %copy-start = (f32[256,256]{1,0:T(8,128)S(1)}, f32[256,256]{1,0:T(8,128)}, u32[]{:S(2)}) copy-start(f32[256,256]{1,0:T(8,128)} %proj_hbm.1) | copy-start | bytes 786436

commit v3 on v2

--- a/solution.py
+++ b/solution.py
@@ -26,6 +26,7 @@
 DY = (2, 1, 3, 0)
 SLOT = {dy: k for k, dy in enumerate(DY)}
 OWN = SLOT[0]
+S_PLANE, S_ROW, S_ENC, S_RS, S_RCOL, S_RROW, S_POS, S_G = range(8)
 
 
 def own_pos(s):
@@ -43,7 +44,7 @@
 
 def kernel(
     proj_hbm, part_hbm, loss_ref, grad_ref,
-    proj_ref, part_ref, u, u32, rows, e, acc, inv, enc, enc_s, pick,
+    proj_ref, part_ref, u, u32, rows, e, acc, inv, enc, index, index_s, pick,
     rs_send, rs_recv, r_cols, r_rows, ri, pos_send, pos_recv, g_own, g_send, g_recv,
     own_sem, sib_sem, row_sem, enc_sem, rs_sem, rcol_sem, rrow_sem, pos_sem, g_sem, send_sem, local_sem, in_sem,
 ):
@@ -57,20 +58,10 @@
         cc = 1 - core if dc else core
         return ((lax.rem(xx, 2) * 4 + zz) * 2 + cc, yy * 2 + xx // 2)
 
-    n_send = [0]
-    sent = []
-
-    def remote(src, dst, recv, to):
-        index = n_send[0]
-        n_send[0] += 1
-
-        def make():
-            return pltpu.make_async_remote_copy(
-                src_ref=src, dst_ref=dst, send_sem=send_sem.at[index], recv_sem=recv, device_id=to, device_id_type=MESH
-            )
-
-        sent.append(make)
-        return make
+    def remote(src, dst, send, recv, to):
+        return pltpu.make_async_remote_copy(
+            src_ref=src, dst_ref=dst, send_sem=send_sem.at[send], recv_sem=recv, device_id=to, device_id_type=MESH
+        )
 
     proj_in = pltpu.make_async_copy(proj_hbm, proj_ref, in_sem.at[0])
     part_in = pltpu.make_async_copy(part_hbm, part_ref, in_sem.at[1])
@@ -91,7 +82,7 @@
     rows[OWN] = low
     part_in.wait()
 
-    p = part_ref[...]
+    p = part_ref[...].reshape(1, BLK)
     off, blk = p & 255, p >> 8
     p_group, p_loop = blk & 7, blk >> 3
     p_x = ((p_group & 1) << 1) + (p_loop >> 3)
@@ -113,8 +104,8 @@
         pltpu.make_async_copy(ref, ref, sem).wait()
 
     line = [(k, DY[k]) for k in range(RING) if DY[k]]
-    row_copies = [remote(u.at[0], rows.at[k], row_sem.at[k], dev(dy=dy)) for k, dy in line]
-    enc_copies = [remote(enc.at[OWN], enc.at[k], enc_sem.at[k], dev(dy=dy)) for k, dy in line]
+    row_copies = [remote(u.at[0], rows.at[k], S_ROW, row_sem, dev(dy=dy)) for k, dy in line]
+    enc_copies = [remote(enc.at[OWN], enc.at[k], S_ENC, enc_sem, dev(dy=dy)) for k, dy in line]
 
     def piece(s, half):
         return u.at[own_pos(s), pl.ds(half * 128, 128), :]
@@ -125,24 +116,24 @@
     def push(s, half, axis, d):
         dx, dz = ORDER[s]
         t = STEP[((dx + d) % 4, dz) if axis == 0 else (dx, (dz + d) % 4)]
-        remote(piece(s, half), piece(t, half), own_sem.at[t, half], dev(dx=d) if axis == 0 else dev(dz=d))().start()
+        remote(piece(s, half), piece(t, half), S_PLANE, own_sem.at[t, half], dev(dx=d) if axis == 0 else dev(dz=d)).start()
 
     def wait_half(s, half):
         wait_for(piece(s, half), own_sem.at[s, half])
 
-    sib_copies = [remote(u.at[own_pos(s)], u.at[sib_pos(s)], sib_sem.at[s], dev(dc=1)) for s in range(16)]
+    sib_copies = [remote(u.at[own_pos(s)], u.at[sib_pos(s)], S_PLANE, sib_sem.at[s], dev(dc=1)) for s in range(16)]
 
     for half in (0, 1):
         for d in (1, 3, 2):
             push(0, half, half, d)
     for k in (1, 2, 0):
-        row_copies[k]().start()
+        row_copies[k].start()
     for half in (0, 1):
         for d in (1, 3, 2):
             push(0, half, 1 - half, d)
-    sib_copies[0]().start()
-    for make in enc_copies:
-        make().start()
+    sib_copies[0].start()
+    for copy in enc_copies:
+        copy.start()
     for d in (1, 3, 2):
         for half in (0, 1):
             s = STEP[along(half, d)]
@@ -151,14 +142,18 @@
                 push(s, half, 1 - half, f)
     for s in range(1, 7):
         wait_half(s, 0 if ORDER[s][0] == 0 else 1)
-        sib_copies[s]().start()
-    for k, dy in line:
-        wait_for(rows.at[k], row_sem.at[k])
+        sib_copies[s].start()
+    wait_for(rows.at[pl.ds(0, 3)], row_sem)
+    wait_for(enc.at[pl.ds(0, 3)], enc_sem)
+    v = enc[...]
+    index[...] = jnp.where((v >> 13) == y, v & (COLS - 1), COLS)
+    to_smem = pltpu.make_async_copy(index, index_s, local_sem)
+    to_smem.start()
 
     def comm_step(s):
         wait_half(s, 0)
         wait_half(s, 1)
-        sib_copies[s]().start()
+        sib_copies[s].start()
 
     scale = inverse_temp * LOG2E
     r_iota = lax.broadcasted_iota(jnp.int32, (BLK, BLK), 0)
@@ -197,16 +192,11 @@
 
     for k in range(RING):
         rs_send[k] = transposed_sum(acc[k])
-    rs_copies = [remote(rs_send.at[k], rs_recv.at[k], rs_sem.at[k], dev(dy=-dy)) for k, dy in line]
-    for make in rs_copies:
-        make().start()
-    for k, dy in line:
-        wait_for(enc.at[k], enc_sem.at[k])
-    to_smem = pltpu.make_async_copy(enc, enc_s, local_sem)
-    to_smem.start()
+    rs_copies = [remote(rs_send.at[k], rs_recv.at[k], S_RS, rs_sem, dev(dy=-dy)) for k, dy in line]
+    for copy in rs_copies:
+        copy.start()
     to_smem.wait()
-    for k, dy in line:
-        wait_for(rs_recv.at[k], rs_sem.at[k])
+    wait_for(rs_recv.at[pl.ds(0, 3)], rs_sem)
     row_sums = rs_send[OWN] + rs_recv[0] + rs_recv[1] + rs_recv[2]
     recip = 1.0 / row_sums
     r_cols[0] = recip
@@ -215,43 +205,37 @@
     for dx, dz, dc in plane:
         s = STEP[(dx, dz)]
         pos = sib_pos(s) if dc else own_pos(s)
-        r_copies.append(remote(r_cols.at[0], r_cols.at[pos], rcol_sem.at[pos], dev(dx, dz, 0, dc)))
+        r_copies.append(remote(r_cols.at[0], r_cols.at[pos], S_RCOL, rcol_sem, dev(dx, dz, 0, dc)))
     for k, dy in line:
-        r_copies.append(remote(r_cols.at[0], r_rows.at[k], rrow_sem.at[k], dev(dy=dy)))
-    for make in r_copies:
-        make().start()
+        r_copies.append(remote(r_cols.at[0], r_rows.at[k], S_RROW, rrow_sem, dev(dy=dy)))
+    for copy in r_copies:
+        copy.start()
 
     for k in range(RING):
 
         def fetch(j, carry):
-            for t in range(8):
-                i = j * 8 + t
-                v = enc_s[k, 0, i]
-                at = jnp.where(v // COLS == y, lax.rem(v, COLS), COLS)
-                pick[k, pl.ds(i, 1), :] = u32[pl.ds(at, 1), :]
+            for t in range(32):
+                i = j * 32 + t
+                pick[k, pl.ds(i, 1), :] = u32[pl.ds(index_s[k, 0, i], 1), :]
             return carry
 
-        lax.fori_loop(0, BLK // 8, fetch, 0)
+        lax.fori_loop(0, BLK // 32, fetch, 0)
     for k in range(RING):
         q = rows[k].astype(F32) * pick[k]
         pos_send[k] = transposed_sum(q[:, :128] + q[:, 128:]) * inverse_temp
-    pos_copies = [remote(pos_send.at[k], pos_recv.at[k], pos_sem.at[k], dev(dy=-dy)) for k, dy in line]
-    for make in pos_copies:
-        make().start()
-
-    for k, dy in line:
-        wait_for(r_rows.at[k], rrow_sem.at[k])
-    for dx, dz, dc in plane:
-        s = STEP[(dx, dz)]
-        pos = sib_pos(s) if dc else own_pos(s)
-        wait_for(r_cols.at[pos], rcol_sem.at[pos])
+    pos_copies = [remote(pos_send.at[k], pos_recv.at[k], S_POS, pos_sem, dev(dy=-dy)) for k, dy in line]
+    for copy in pos_copies:
+        copy.start()
+
+    wait_for(r_rows.at[pl.ds(0, 3)], rrow_sem)
+    wait_for(r_cols.at[pl.ds(1, PLANE - 1)], rcol_sem)
     for k in range(RING):
         r = r_rows[k]
         for h in (0, 1):
             part = jnp.broadcast_to(r[:, h * 128 : (h + 1) * 128], (128, 128))
             ri[k, h * 128 : (h + 1) * 128, :] = jnp.transpose(part)
 
-    g_copies = [remote(g_send.at[k], g_recv.at[k], g_sem.at[k], dev(dy=-dy)) for k, dy in line]
+    g_copies = [remote(g_send.at[k], g_recv.at[k], S_G, g_sem, dev(dy=-dy)) for k, dy in line]
 
     def weigh(k, carry):
         r_row = jnp.concatenate([ri[k], ri[k]], axis=1)
@@ -266,29 +250,28 @@
 
             @pl.when(k == t)
             def _():
-                g_copies[t]().start()
+                g_copies[t].start()
 
         return carry
 
     lax.fori_loop(0, RING, weigh, 0)
 
-    for k, dy in line:
-        wait_for(pos_recv.at[k], pos_sem.at[k])
+    wait_for(pos_recv.at[pl.ds(0, 3)], pos_sem)
     positive = pos_send[OWN] + pos_recv[0] + pos_recv[1] + pos_recv[2]
-    loss_ref[...] = jnp.log(row_sums) - positive
-    for k, dy in line:
-        wait_for(g_recv.at[k], g_sem.at[k])
+    loss_ref[...] = (jnp.log(row_sums) - positive).reshape(BLK)
+    wait_for(g_recv.at[pl.ds(0, 3)], g_sem)
     grad_unit = g_own[...] + g_recv[0].astype(F32) + g_recv[1].astype(F32) + g_recv[2].astype(F32)
     inv_b = jnp.concatenate([inv[...], inv[...]], axis=1)
     unit = proj_ref[...] * inv_b
     along = jnp.sum(unit * grad_unit, axis=1, keepdims=True)
     grad_ref[...] = inv_b * (grad_unit - unit * along)
 
-    for make in sent:
-        make().wait_send()
-
-
-N_SEND = 150
+    wait_for(u.at[pl.ds(0, 31)], send_sem.at[S_PLANE])
+    for sem, ref in (
+        (S_ROW, rows), (S_ENC, enc), (S_RS, rs_send), (S_RROW, r_rows), (S_POS, pos_send), (S_G, g_send),
+    ):
+        wait_for(ref.at[pl.ds(0, 3)], send_sem.at[sem])
+    wait_for(r_cols.at[pl.ds(1, PLANE - 1)], send_sem.at[S_RCOL])
 
 
 def on_device(projections, partners):
@@ -296,12 +279,12 @@
     vmem = pl.BlockSpec(memory_space=pltpu.VMEM)
     loss, grad = pl.pallas_call(
         kernel,
-        out_shape=(jax.ShapeDtypeStruct((1, BLK), F32), jax.ShapeDtypeStruct((BLK, PROJ), F32)),
+        out_shape=(jax.ShapeDtypeStruct((BLK,), F32), jax.ShapeDtypeStruct((BLK, PROJ), F32)),
         in_specs=[pl.BlockSpec(memory_space=pltpu.HBM)] * 2,
         out_specs=(vmem, vmem),
         scratch_shapes=[
             pltpu.VMEM((BLK, PROJ), F32),
-            pltpu.VMEM((1, BLK), jnp.int32),
+            pltpu.VMEM((BLK,), jnp.int32),
             pltpu.VMEM((PLANE, BLK, PROJ), BF16),
             pltpu.VMEM((COLS + 8, PROJ), F32),
             pltpu.VMEM((RING, BLK, PROJ), BF16),
@@ -309,6 +292,7 @@
             pltpu.VMEM((RING, BLK, 128), F32),
             pltpu.VMEM((BLK, 128), F32),
             pltpu.VMEM((RING, 1, BLK), jnp.int32),
+            pltpu.VMEM((RING, 1, BLK), jnp.int32),
             pltpu.SMEM((RING, 1, BLK), jnp.int32),
             pltpu.VMEM((RING, BLK, PROJ), F32),
             pltpu.VMEM((RING, 1, BLK), F32),
@@ -321,15 +305,14 @@
             pltpu.VMEM((BLK, PROJ), F32),
             pltpu.VMEM((RING, BLK, PROJ), BF16),
             pltpu.VMEM((RING, BLK, PROJ), BF16),
-            dma((16, 2)), dma((16,)), dma((3,)), dma((3,)), dma((3,)), dma((PLANE,)), dma((3,)), dma((3,)), dma((3,)),
-            dma((N_SEND,)), dma, dma((2,)),
+            dma((16, 2)), dma((16,)), dma, dma, dma, dma, dma, dma, dma, dma((8,)), dma, dma((2,)),
         ],
         compiler_params=pltpu.CompilerParams(
-            collective_id=0, has_side_effects=True, vmem_limit_bytes=48 * 1024 * 1024
+            collective_id=0, has_side_effects=True, vmem_limit_bytes=54850 * 1024
         ),
         cost_estimate=pl.CostEstimate(flops=4 * ROWS * COLS * PROJ, bytes_accessed=8 << 20, transcendentals=ROWS * COLS),
-    )(projections, partners.reshape(1, BLK))
-    return loss.reshape(BLK), grad
+    )(projections, partners)
+    return loss, grad
 
 
 def solution(mesh):

time: 56.5 us -> 48.3 us (0.85)
  Pallas kernels: 52.6 us -> 45.3 us
  local copies, waits for them, and re-layouts: 2.89 us -> 1.94 us
    pallas_call x1, Pallas kernels: 52.6 us -> 45.3 us  [on_device(): pl.pallas_call(kernel, out_shape=(jax.ShapeDtypeStruct((BLK,), F32), jax....]
    unnamed x6 -> x4, local copies, waits for them, and re-layouts: 2.89 us -> 1.94 us
where the time goes in v3:
time: 48.3 us; the launch traced here: 47.9 us
  Pallas kernels  45.3 us (94%)
  local copies, waits for them, and re-layouts  1.94 us (4%)
  between operations  0.65 us (1%)
    pallas_call x1, Pallas kernels, on_device(): pl.pallas_call(kernel, out_shape=(jax.ShapeDtypeStruct((BLK,), F32), jax....  45.3 us
    unnamed x4, local copies, waits for them, and re-layouts  1.94 us

profile of v3, /device:TPU:0, one launch (start us, length us, event | category | flops | bytes accessed | tf_op | source)
XLA Modules:
  0.0 47.9 jit_solution(16075656644477633428)
XLA Ops:
  0.6 0.0 copy-start
  0.6 0.7 %copy-done = s32[256]{0:T(256)S(1)} copy-done((s32[256]{0:T(256)S(1)}, s32[256]{0:T(256)}, u32[]{:S(2)}) %copy-start) | copy-done | bytes 1048
  1.3 45.3 %shard_map.41 = (f32[256]{0:T(256)S(1)}, f32[256,256]{1,0:T(8,128)S(1)}) custom-call(f32[256,256]{1,0:T(8,128)} %proj_hbm.1, s32[256]{0:T(256)S(1)} %copy-done), custom_call_target="tpu_custom_call" | custom-call | flops 8589934592 | bytes 8388608 | tf_op jit(solution)/shard_map/pallas_call | solution.py:280
  46.6 0.6 %copy.6 = f32[256]{0:T(256)} copy(f32[256]{0:T(256)S(1)} %get-tuple-element.4) | data formatting | bytes 2048
  47.2 0.7 %copy.7 = f32[256,256]{1,0:T(8,128)} copy(f32[256,256]{1,0:T(8,128)S(1)} %get-tuple-element.5) | data formatting | bytes 524288
Async XLA Ops:
  0.6 0.7 %copy-start = (s32[256]{0:T(256)S(1)}, s32[256]{0:T(256)}, u32[]{:S(2)}) copy-start(s32[256]{0:T(256)} %part_hbm.1) | copy-start | bytes 3076

commit v4 on v3

v4 whole, which is shorter than its diff:
```python
import jax
import jax.numpy as jnp
from jax import lax
from jax.experimental import pallas as pl
from jax.experimental.pallas import tpu as pltpu
from jax.sharding import PartitionSpec as P

MESH = pl.DeviceIdType.MESH
F32, BF16 = jnp.float32, jnp.bfloat16
epsilon = 1e-06
inverse_temp = 10.0
LOG2E = 1.4426950408889634

PROJ = 256
BLK = 256
RING = 4
PLANE = RING * RING
COLS = PLANE * BLK
LINE = 2 * RING

ORDER = [
    (0, 0), (1, 0), (0, 1), (3, 0), (0, 3), (2, 0), (0, 2), (1, 1),
    (3, 1), (1, 3), (3, 3), (1, 2), (3, 2), (2, 1), (2, 3), (2, 2),
]
STEP = {d: s for s, d in enumerate(ORDER)}
SLOTS = ((1, 2), (1, 1), (0, 2), (1, 3), (0, 1), (1, 0), (0, 3), (0, 0))
OWN = 7
TWOS = 7
FIRST = 3
LINE_DY = (2, 1, 3, 0)
S_PLANE, S_ROW, S_ENC, S_RS, S_RCOL, S_RROW, S_POS, S_G, S_SIB = range(9)


def transposed_sum(v):
    parts = [jnp.sum(jnp.transpose(v[i * 128 : (i + 1) * 128, :]), axis=0, keepdims=True) for i in range(2)]
    return jnp.concatenate(parts, axis=1)


def kernel(
    proj_hbm, part_hbm, loss_ref, grad_ref,
    proj_ref, part_ref, u, u32, rows, e, acc, inv, enc, index, index_s, pick,
    rs_send, rs_recv, r_cols, r_rows, ri, pos_send, pos_recv, g_own, g_send, g_recv, s_send, s_recv,
    own_sem, row_sem, row_sib_sem, enc_sem, rs_sem, rcol_sem, rrow_sem, pos_sem, g_sem, s_sem, send_sem, local_sem, in_sem,
):
    loop, group = lax.axis_index("loop"), lax.axis_index("group")
    core, z, x_lo = lax.rem(loop, 2), lax.rem(loop // 2, 4), loop // 8
    y, x_hi = group // 2, lax.rem(group, 2)
    x = x_hi * 2 + x_lo

    def dev(dx=0, dz=0, dy=0, dc=0):
        xx, zz, yy = lax.rem(x + dx + 4, 4), lax.rem(z + dz + 4, 4), lax.rem(y + dy + 4, 4)
        cc = 1 - core if dc else core
        return ((lax.rem(xx, 2) * 4 + zz) * 2 + cc, yy * 2 + xx // 2)

    def remote(src, dst, send, recv, to):
        return pltpu.make_async_remote_copy(
            src_ref=src, dst_ref=dst, send_sem=send_sem.at[send], recv_sem=recv, device_id=to, device_id_type=MESH
        )

    proj_in = pltpu.make_async_copy(proj_hbm, proj_ref, in_sem.at[0])
    part_in = pltpu.make_async_copy(part_hbm, part_ref, in_sem.at[1])
    proj_in.start()
    part_in.start()
    plane = [(dx, dz) for dz in (2, 1, 3, 0) for dx in (2, 1, 3, 0) if (dx, dz) != (0, 0)]
    line = [(j, dc, dy) for j, (dc, dy) in enumerate(SLOTS) if j != OWN]
    near = [dev(dx=k) for k in (1, 2, 3)] + [dev(dz=k) for k in (1, 2, 3)] + [dev(dy=k) for k in (1, 2, 3)] + [dev(dc=1)]
    barrier = pltpu.get_barrier_semaphore()
    for to in near:
        pl.semaphore_signal(barrier, inc=1, device_id=to, device_id_type=MESH)

    proj_in.wait()
    proj = proj_ref[...]
    inv_norm = lax.rsqrt(jnp.sum(proj * proj, axis=1, keepdims=True) + epsilon)
    inv[...] = jnp.broadcast_to(inv_norm, inv.shape)
    low = (proj * inv_norm).astype(BF16)
    u[0] = low
    rows[OWN] = low
    part_in.wait()

    p = part_ref[...].reshape(1, BLK)
    off, blk = p & 255, p >> 8
    p_group, p_loop = blk & 7, blk >> 3
    p_x = ((p_group & 1) << 1) + (p_loop >> 3)
    p_z, p_c = (p_loop >> 1) & 3, p_loop & 1
    key = ((x - p_x) & 3) * 4 + ((z - p_z) & 3)
    place = jnp.zeros_like(p)
    for d, t in STEP.items():
        place = jnp.where(key == d[0] * 4 + d[1], t, place)
    enc[OWN] = ((p_group >> 1) * 2 + p_c) * COLS + place * BLK + off
    u32[COLS : COLS + 8, :] = jnp.zeros((8, PROJ), F32)
    acc[...] = jnp.zeros_like(acc)

    pl.semaphore_wait(barrier, len(near))

    def wait_for(ref, sem):
        pltpu.make_async_copy(ref, ref, sem).wait()

    def row_copy(dy):
        t = SLOTS.index((0, dy))
        return remote(u.at[0], rows.at[t], S_ROW, row_sem.at[LINE_DY.index(dy)], dev(dy=dy))

    def row_to_sib(dy):
        return remote(rows.at[SLOTS.index((0, dy))], rows.at[SLOTS.index((1, dy))], S_ROW, row_sib_sem, dev(dc=1))

    def row_arrived(dy):
        wait_for(rows.at[SLOTS.index((0, dy))], row_sem.at[LINE_DY.index(dy)])

    def piece(s, half):
        return u.at[s, pl.ds(half * 128, 128), :]

    def along(half, d):
        return (d, 0) if half == 0 else (0, d)

    def push(s, half, axis, d):
        dx, dz = ORDER[s]
        t = STEP[((dx + d) % 4, dz) if axis == 0 else (dx, (dz + d) % 4)]
        remote(piece(s, half), piece(t, half), S_PLANE, own_sem.at[t, half], dev(dx=d) if axis == 0 else dev(dz=d)).start()

    def wait_half(s, half):
        wait_for(piece(s, half), own_sem.at[s, half])

    for half in (0, 1):
        for d in (1, 3):
            push(0, half, half, d)
    for half in (0, 1):
        push(0, half, half, 2)
    for dy in (1, 3, 2):
        row_copy(dy).start()
    for half in (1, 0):
        for d in (1, 3, 2):
            push(0, half, 1 - half, d)
    row_to_sib(0).start()
    for d in (1, 3, 2):
        for half in (0, 1):
            s = STEP[along(half, d)]
            wait_half(s, half)
            for f in (1, 3, 2):
                push(s, half, 1 - half, f)
        row_arrived(d)
        row_to_sib(d).start()
    wait_for(rows.at[pl.ds(0, 4)], row_sib_sem)
    for j, dc, dy in line:
        remote(enc.at[OWN], enc.at[j], S_ENC, enc_sem, dev(dy=dy, dc=dc)).start()

    scale = inverse_temp * LOG2E
    r_iota = lax.broadcasted_iota(jnp.int32, (BLK, BLK), 0)
    c_iota = lax.broadcasted_iota(jnp.int32, (BLK, BLK), 1)

    def arrive(i):
        @pl.when((i >= 1) & (i < 7))
        def _():
            half = lax.rem(i, 2)
            wait_for(u.at[i, pl.ds(pl.multiple_of(half * 128, 128), 128), :], own_sem.at[i, half])

        @pl.when(i >= 7)
        def _():
            wait_half(i, 0)
            wait_half(i, 1)

    def compute(blocks):
        for i in blocks:
            arrive(i)
        for i in blocks:
            block = u[i]
            u32[pl.ds(pl.multiple_of(i * BLK, BLK), BLK), :] = block.astype(F32)
            for j in range(LINE):
                dots = lax.dot_general(rows[j], block, (((1,), (1,)), ((), ())), preferred_element_type=F32)
                ex = jnp.exp2(dots * scale)
                if j == OWN:
                    ex = jnp.where(r_iota == c_iota + i * BLK, 0.0, ex)
                acc[j] += ex[:, :128] + ex[:, 128:]
                e[j, i] = ex.astype(BF16)

    def two(n, carry):
        compute((2 * n, 2 * n + 1))
        return carry

    def one(i, carry):
        compute((i,))
        return carry

    lax.fori_loop(0, TWOS, two, 0)
    lax.fori_loop(2 * TWOS, PLANE, one, 0)

    for j in range(LINE):
        rs_send[j] = transposed_sum(acc[j])
    for j, dc, dy in line:
        remote(rs_send.at[j], rs_recv.at[j], S_RS, rs_sem, dev(dy=-dy, dc=dc)).start()

    wait_for(enc.at[pl.ds(0, 7)], enc_sem)
    v = enc[...]
    index[...] = jnp.where((v >> 12) == y * 2 + core, v & (COLS - 1), COLS)
    to_smem = pltpu.make_async_copy(index, index_s, local_sem)
    to_smem.start()
    to_smem.wait()

    def fetch(j, carry):
        for t in range(BLK):
            pick[j, t : t + 1, :] = u32[pl.ds(index_s[j, 0, t], 1), :]
        return carry

    lax.fori_loop(0, FIRST, fetch, 0)

    wait_for(rs_recv.at[pl.ds(0, 7)], rs_sem)
    row_sums = rs_send[OWN]
    for j, dc, dy in line:
        row_sums += rs_recv[j]
    recip = 1.0 / row_sums
    r_cols[0] = recip
    r_rows[OWN] = recip
    for dx, dz in plane:
        remote(r_cols.at[0], r_cols.at[STEP[(dx, dz)]], S_RCOL, rcol_sem, dev(dx, dz)).start()
    for j, dc, dy in line:
        remote(r_cols.at[0], r_rows.at[j], S_RROW, rrow_sem, dev(dy=dy, dc=dc)).start()

    lax.fori_loop(FIRST, LINE, fetch, 0)
    for j in range(LINE):
        q = rows[j].astype(F32) * pick[j]
        pos_send[j] = transposed_sum(q[:, :128] + q[:, 128:]) * inverse_temp
    for j, dc, dy in line:
        remote(pos_send.at[j], pos_recv.at[j], S_POS, pos_sem, dev(dy=-dy, dc=dc)).start()

    wait_for(r_rows.at[pl.ds(0, 7)], rrow_sem)
    for j in range(LINE):
        r = r_rows[j]
        for h in (0, 1):
            part = jnp.broadcast_to(r[:, h * 128 : (h + 1) * 128], (128, 128))
            ri[j, h * 128 : (h + 1) * 128, :] = jnp.transpose(part)
    wait_for(r_cols.at[pl.ds(1, PLANE - 1)], rcol_sem)

    def weigh(j, carry):
        r_row = jnp.concatenate([ri[j], ri[j]], axis=1)
        total = jnp.zeros((BLK, PROJ), F32)
        for pos in range(PLANE):
            w = e[j, pos].astype(F32) * (r_row + r_cols[pos])
            total += jnp.dot(w.astype(BF16), u[pos], preferred_element_type=F32)
        g_own[...] = inverse_temp * (total - 2.0 * pick[j])
        for t, (dc, dy) in enumerate(SLOTS):

            @pl.when(j == t)
            def _():
                k = LINE_DY.index(dy)
                if dc:
                    s_send[k] = g_own[...].astype(BF16)
                    remote(s_send.at[k], s_recv.at[k], S_SIB, s_sem.at[k], dev(dc=1)).start()
                else:
                    wait_for(s_recv.at[k], s_sem.at[k])
                    if dy:
                        g_send[k] = (g_own[...] + s_recv[k].astype(F32)).astype(BF16)
                        remote(g_send.at[k], g_recv.at[k], S_G, g_sem, dev(dy=-dy)).start()

        return carry

    lax.fori_loop(0, LINE, weigh, 0)

    wait_for(pos_recv.at[pl.ds(0, 7)], pos_sem)
    positive = pos_send[OWN]
    for j, dc, dy in line:
        positive += pos_recv[j]
    loss_ref[...] = (jnp.log(row_sums) - positive).reshape(BLK)
    wait_for(g_recv.at[pl.ds(0, 3)], g_sem)
    grad_unit = g_own[...] + s_recv[3].astype(F32) + g_recv[0].astype(F32) + g_recv[1].astype(F32) + g_recv[2].astype(F32)
    inv_b = jnp.concatenate([inv[...], inv[...]], axis=1)
    unit = proj_ref[...] * inv_b
    along = jnp.sum(unit * grad_unit, axis=1, keepdims=True)
    grad_ref[...] = inv_b * (grad_unit - unit * along)

    for sem, ref, n in (
        (S_PLANE, u, 15), (S_ROW, rows, 7), (S_ENC, enc, 7), (S_RS, rs_send, 7), (S_RCOL, r_cols, 15), (S_RROW, r_rows, 7),
        (S_POS, pos_send, 7), (S_G, g_send, 3), (S_SIB, s_send, 4),
    ):
        wait_for(ref.at[pl.ds(0, n)], send_sem.at[sem])


def on_device(projections, partners):
    dma = pltpu.SemaphoreType.DMA
    vmem = pl.BlockSpec(memory_space=pltpu.VMEM)
    loss, grad = pl.pallas_call(
        kernel,
        out_shape=(jax.ShapeDtypeStruct((BLK,), F32), jax.ShapeDtypeStruct((BLK, PROJ), F32)),
        in_specs=[pl.BlockSpec(memory_space=pltpu.HBM)] * 2,
        out_specs=(vmem, vmem),
        scratch_shapes=[
            pltpu.VMEM((BLK, PROJ), F32),
            pltpu.VMEM((BLK,), jnp.int32),
            pltpu.VMEM((PLANE, BLK, PROJ), BF16),
            pltpu.VMEM((COLS + 8, PROJ), F32),
            pltpu.VMEM((LINE, BLK, PROJ), BF16),
            pltpu.VMEM((LINE, PLANE, BLK, BLK), BF16),
            pltpu.VMEM((LINE, BLK, 128), F32),
            pltpu.VMEM((BLK, 128), F32),
            pltpu.VMEM((LINE, 1, BLK), jnp.int32),
            pltpu.VMEM((LINE, 1, BLK), jnp.int32),
            pltpu.SMEM((LINE, 1, BLK), jnp.int32),
            pltpu.VMEM((LINE, BLK, PROJ), F32),
            pltpu.VMEM((LINE, 1, BLK), F32),
            pltpu.VMEM((LINE, 1, BLK), F32),
            pltpu.VMEM((PLANE, 1, BLK), F32),
            pltpu.VMEM((LINE, 1, BLK), F32),
            pltpu.VMEM((LINE, BLK, 128), F32),
            pltpu.VMEM((LINE, 1, BLK), F32),
            pltpu.VMEM((LINE, 1, BLK), F32),
            pltpu.VMEM((BLK, PROJ), F32),
            pltpu.VMEM((RING, BLK, PROJ), BF16),
            pltpu.VMEM((RING, BLK, PROJ), BF16),
            pltpu.VMEM((RING, BLK, PROJ), BF16),
            pltpu.VMEM((RING, BLK, PROJ), BF16),
            dma((16, 2)), dma((3,)), dma, dma, dma, dma, dma, dma, dma, dma((RING,)), dma((9,)), dma, dma((2,)),
        ],
        compiler_params=pltpu.CompilerParams(
            collective_id=0, has_side_effects=True, vmem_limit_bytes=54850 * 1024
        ),
        cost_estimate=pl.CostEstimate(flops=4 * LINE * BLK * COLS * PROJ, bytes_accessed=8 << 20, transcendentals=LINE * BLK * COLS),
    )(projections, partners)
    return loss, grad


def solution(mesh):
    return jax.shard_map(
        on_device,
        mesh=mesh,
        in_specs=(P(("loop", "group"), None), P(("loop", "group"))),
        out_specs=(P(("loop", "group")), P(("loop", "group"), None)),
        check_vma=False,
    )
```

time: 48.3 us -> 47.1 us (0.975)
  Pallas kernels: 45.3 us -> 44 us
    pallas_call x1, Pallas kernels: 45.3 us -> 44 us  [on_device(): pl.pallas_call(kernel, out_shape=(jax.ShapeDtypeStruct((BLK,), F32), jax....]
where the time goes in v4:
time: 47.1 us; the launch traced here: 46.6 us
  Pallas kernels  44 us (93%)
  local copies, waits for them, and re-layouts  1.94 us (4%)
  between operations  0.65 us (1%)
    pallas_call x1, Pallas kernels, on_device(): pl.pallas_call(kernel, out_shape=(jax.ShapeDtypeStruct((BLK,), F32), jax....  44 us
    unnamed x4, local copies, waits for them, and re-layouts  1.94 us

profile of v4, /device:TPU:0, one launch (start us, length us, event | category | flops | bytes accessed | tf_op | source)
XLA Modules:
  0.0 46.6 jit_solution(7454493203621979216)
XLA Ops:
  0.6 0.0 copy-start
  0.6 0.7 %copy-done = s32[256]{0:T(256)S(1)} copy-done((s32[256]{0:T(256)S(1)}, s32[256]{0:T(256)}, u32[]{:S(2)}) %copy-start) | copy-done | bytes 1048
  1.3 44.0 %shard_map.41 = (f32[256]{0:T(256)S(1)}, f32[256,256]{1,0:T(8,128)S(1)}) custom-call(f32[256,256]{1,0:T(8,128)} %proj_hbm.1, s32[256]{0:T(256)S(1)} %copy-done), custom_call_target="tpu_custom_call" | custom-call | flops 8589934592 | bytes 8388608 | tf_op jit(solution)/shard_map/pallas_call | solution.py:278
  45.3 0.6 %copy.6 = f32[256]{0:T(256)} copy(f32[256]{0:T(256)S(1)} %get-tuple-element.4) | data formatting | bytes 2048
  45.9 0.7 %copy.7 = f32[256,256]{1,0:T(8,128)} copy(f32[256,256]{1,0:T(8,128)S(1)} %get-tuple-element.5) | data formatting | bytes 524288
Async XLA Ops:
  0.6 0.7 %copy-start = (s32[256]{0:T(256)S(1)}, s32[256]{0:T(256)}, u32[]{:S(2)}) copy-start(s32[256]{0:T(256)} %part_hbm.1) | copy-start | bytes 3076

commit v5 on v4

--- a/solution.py
+++ b/solution.py
@@ -23,12 +23,11 @@
     (3, 1), (1, 3), (3, 3), (1, 2), (3, 2), (2, 1), (2, 3), (2, 2),
 ]
 STEP = {d: s for s, d in enumerate(ORDER)}
-SLOTS = ((1, 2), (1, 1), (0, 2), (1, 3), (0, 1), (1, 0), (0, 3), (0, 0))
+SLOTS = ((1, 2), (0, 2), (1, 1), (0, 1), (1, 3), (0, 3), (1, 0), (0, 0))
 OWN = 7
 TWOS = 7
 FIRST = 3
-LINE_DY = (2, 1, 3, 0)
-S_PLANE, S_ROW, S_ENC, S_RS, S_RCOL, S_RROW, S_POS, S_G, S_SIB = range(9)
+S_PLANE, S_ROW, S_ENC, S_RS, S_RCOL, S_RROW, S_POS, S_G = range(8)
 
 
 def transposed_sum(v):
@@ -39,18 +38,25 @@
 def kernel(
     proj_hbm, part_hbm, loss_ref, grad_ref,
     proj_ref, part_ref, u, u32, rows, e, acc, inv, enc, index, index_s, pick,
-    rs_send, rs_recv, r_cols, r_rows, ri, pos_send, pos_recv, g_own, g_send, g_recv, s_send, s_recv,
-    own_sem, row_sem, row_sib_sem, enc_sem, rs_sem, rcol_sem, rrow_sem, pos_sem, g_sem, s_sem, send_sem, local_sem, in_sem,
+    rs_send, rs_recv, r_cols, r_rows, ri, pos_send, pos_recv, g_own, g_send, g_recv,
+    own_sem, row_sem, enc_sem, rs_sem, rcol_sem, rrow_sem, pos_sem, g_sem, send_sem, local_sem, in_sem,
 ):
     loop, group = lax.axis_index("loop"), lax.axis_index("group")
     core, z, x_lo = lax.rem(loop, 2), lax.rem(loop // 2, 4), loop // 8
     y, x_hi = group // 2, lax.rem(group, 2)
     x = x_hi * 2 + x_lo
 
-    def dev(dx=0, dz=0, dy=0, dc=0):
-        xx, zz, yy = lax.rem(x + dx + 4, 4), lax.rem(z + dz + 4, 4), lax.rem(y + dy + 4, 4)
+    first = core == 0
+    p, q = jnp.where(first, x, y), jnp.where(first, y, x)
+
+    def dev(dp=0, dz=0, dq=0, dc=0):
+        pp, qq, zz = lax.rem(p + dp + 4, 4), lax.rem(q + dq + 4, 4), lax.rem(z + dz + 4, 4)
+        xx, yy = jnp.where(first, pp, qq), jnp.where(first, qq, pp)
         cc = 1 - core if dc else core
         return ((lax.rem(xx, 2) * 4 + zz) * 2 + cc, yy * 2 + xx // 2)
+
+    def reader(dc, dq):
+        return dev(dp=dq, dc=1) if dc else dev(dq=dq)
 
     def remote(src, dst, send, recv, to):
         return pltpu.make_async_remote_copy(
@@ -62,8 +68,9 @@
     proj_in.start()
     part_in.start()
     plane = [(dx, dz) for dz in (2, 1, 3, 0) for dx in (2, 1, 3, 0) if (dx, dz) != (0, 0)]
-    line = [(j, dc, dy) for j, (dc, dy) in enumerate(SLOTS) if j != OWN]
-    near = [dev(dx=k) for k in (1, 2, 3)] + [dev(dz=k) for k in (1, 2, 3)] + [dev(dy=k) for k in (1, 2, 3)] + [dev(dc=1)]
+    line = [(j, dc, dq) for j, (dc, dq) in enumerate(SLOTS) if j != OWN]
+    near = [dev(dp=k) for k in (1, 2, 3)] + [dev(dz=k) for k in (1, 2, 3)] + [dev(dq=k) for k in (1, 2, 3)]
+    near += [dev(dq=k, dc=1) for k in (0, 1, 2, 3)]
     barrier = pltpu.get_barrier_semaphore()
     for to in near:
         pl.semaphore_signal(barrier, inc=1, device_id=to, device_id_type=MESH)
@@ -77,16 +84,7 @@
     rows[OWN] = low
     part_in.wait()
 
-    p = part_ref[...].reshape(1, BLK)
-    off, blk = p & 255, p >> 8
-    p_group, p_loop = blk & 7, blk >> 3
-    p_x = ((p_group & 1) << 1) + (p_loop >> 3)
-    p_z, p_c = (p_loop >> 1) & 3, p_loop & 1
-    key = ((x - p_x) & 3) * 4 + ((z - p_z) & 3)
-    place = jnp.zeros_like(p)
-    for d, t in STEP.items():
-        place = jnp.where(key == d[0] * 4 + d[1], t, place)
-    enc[OWN] = ((p_group >> 1) * 2 + p_c) * COLS + place * BLK + off
+    enc[OWN] = part_ref[...].reshape(1, BLK)
     u32[COLS : COLS + 8, :] = jnp.zeros((8, PROJ), F32)
     acc[...] = jnp.zeros_like(acc)
 
@@ -94,16 +92,6 @@
 
     def wait_for(ref, sem):
         pltpu.make_async_copy(ref, ref, sem).wait()
-
-    def row_copy(dy):
-        t = SLOTS.index((0, dy))
-        return remote(u.at[0], rows.at[t], S_ROW, row_sem.at[LINE_DY.index(dy)], dev(dy=dy))
-
-    def row_to_sib(dy):
-        return remote(rows.at[SLOTS.index((0, dy))], rows.at[SLOTS.index((1, dy))], S_ROW, row_sib_sem, dev(dc=1))
-
-    def row_arrived(dy):
-        wait_for(rows.at[SLOTS.index((0, dy))], row_sem.at[LINE_DY.index(dy)])
 
     def piece(s, half):
         return u.at[s, pl.ds(half * 128, 128), :]
@@ -114,7 +102,7 @@
     def push(s, half, axis, d):
         dx, dz = ORDER[s]
         t = STEP[((dx + d) % 4, dz) if axis == 0 else (dx, (dz + d) % 4)]
-        remote(piece(s, half), piece(t, half), S_PLANE, own_sem.at[t, half], dev(dx=d) if axis == 0 else dev(dz=d)).start()
+        remote(piece(s, half), piece(t, half), S_PLANE, own_sem.at[t, half], dev(dp=d) if axis == 0 else dev(dz=d)).start()
 
     def wait_half(s, half):
         wait_for(piece(s, half), own_sem.at[s, half])
@@ -124,23 +112,22 @@
             push(0, half, half, d)
     for half in (0, 1):
         push(0, half, half, 2)
-    for dy in (1, 3, 2):
-        row_copy(dy).start()
+    for dq in (1, 3, 2, 0):
+        for dc in (0, 1):
+            if (dc, dq) != (0, 0):
+                remote(u.at[0], rows.at[SLOTS.index((dc, dq))], S_ROW, row_sem, reader(dc, dq)).start()
     for half in (1, 0):
         for d in (1, 3, 2):
             push(0, half, 1 - half, d)
-    row_to_sib(0).start()
     for d in (1, 3, 2):
         for half in (0, 1):
             s = STEP[along(half, d)]
             wait_half(s, half)
             for f in (1, 3, 2):
                 push(s, half, 1 - half, f)
-        row_arrived(d)
-        row_to_sib(d).start()
-    wait_for(rows.at[pl.ds(0, 4)], row_sib_sem)
-    for j, dc, dy in line:
-        remote(enc.at[OWN], enc.at[j], S_ENC, enc_sem, dev(dy=dy, dc=dc)).start()
+    for j, dc, dq in line:
+        remote(enc.at[OWN], enc.at[j], S_ENC, enc_sem, reader(dc, dq)).start()
+    wait_for(rows.at[pl.ds(0, 7)], row_sem)
 
     scale = inverse_temp * LOG2E
     r_iota = lax.broadcasted_iota(jnp.int32, (BLK, BLK), 0)
@@ -184,12 +171,19 @@
 
     for j in range(LINE):
         rs_send[j] = transposed_sum(acc[j])
-    for j, dc, dy in line:
-        remote(rs_send.at[j], rs_recv.at[j], S_RS, rs_sem, dev(dy=-dy, dc=dc)).start()
+    for j, dc, dq in line:
+        remote(rs_send.at[j], rs_recv.at[j], S_RS, rs_sem, dev(dq=-dq, dc=dc)).start()
 
     wait_for(enc.at[pl.ds(0, 7)], enc_sem)
     v = enc[...]
-    index[...] = jnp.where((v >> 12) == y * 2 + core, v & (COLS - 1), COLS)
+    off, v_group, v_loop = v & 255, (v >> 8) & 7, v >> 11
+    v_x, v_y = ((v_group & 1) << 1) + (v_loop >> 3), v_group >> 1
+    v_p, v_q = jnp.where(first, v_x, v_y), jnp.where(first, v_y, v_x)
+    key = ((p - v_p) & 3) * 4 + ((z - (v_loop >> 1)) & 3)
+    place = jnp.zeros_like(v)
+    for d, t in STEP.items():
+        place = jnp.where(key == d[0] * 4 + d[1], t, place)
+    index[...] = jnp.where(((v_loop & 1) == core) & (v_q == q), place * BLK + off, COLS)
     to_smem = pltpu.make_async_copy(index, index_s, local_sem)
     to_smem.start()
     to_smem.wait()
@@ -203,22 +197,22 @@
 
     wait_for(rs_recv.at[pl.ds(0, 7)], rs_sem)
     row_sums = rs_send[OWN]
-    for j, dc, dy in line:
+    for j, dc, dq in line:
         row_sums += rs_recv[j]
     recip = 1.0 / row_sums
     r_cols[0] = recip
     r_rows[OWN] = recip
     for dx, dz in plane:
         remote(r_cols.at[0], r_cols.at[STEP[(dx, dz)]], S_RCOL, rcol_sem, dev(dx, dz)).start()
-    for j, dc, dy in line:
-        remote(r_cols.at[0], r_rows.at[j], S_RROW, rrow_sem, dev(dy=dy, dc=dc)).start()
+    for j, dc, dq in line:
+        remote(r_cols.at[0], r_rows.at[j], S_RROW, rrow_sem, reader(dc, dq)).start()
 
     lax.fori_loop(FIRST, LINE, fetch, 0)
     for j in range(LINE):
-        q = rows[j].astype(F32) * pick[j]
-        pos_send[j] = transposed_sum(q[:, :128] + q[:, 128:]) * inverse_temp
-    for j, dc, dy in line:
-        remote(pos_send.at[j], pos_recv.at[j], S_POS, pos_sem, dev(dy=-dy, dc=dc)).start()
+        both = rows[j].astype(F32) * pick[j]
+        pos_send[j] = transposed_sum(both[:, :128] + both[:, 128:]) * inverse_temp
+    for j, dc, dq in line:
+        remote(pos_send.at[j], pos_recv.at[j], S_POS, pos_sem, dev(dq=-dq, dc=dc)).start()
 
     wait_for(r_rows.at[pl.ds(0, 7)], rrow_sem)
     for j in range(LINE):
@@ -235,19 +229,12 @@
             w = e[j, pos].astype(F32) * (r_row + r_cols[pos])
             total += jnp.dot(w.astype(BF16), u[pos], preferred_element_type=F32)
         g_own[...] = inverse_temp * (total - 2.0 * pick[j])
-        for t, (dc, dy) in enumerate(SLOTS):
+        g_send[j] = g_own[...].astype(BF16)
+        for t, dc, dq in line:
 
             @pl.when(j == t)
             def _():
-                k = LINE_DY.index(dy)
-                if dc:
-                    s_send[k] = g_own[...].astype(BF16)
-                    remote(s_send.at[k], s_recv.at[k], S_SIB, s_sem.at[k], dev(dc=1)).start()
-                else:
-                    wait_for(s_recv.at[k], s_sem.at[k])
-                    if dy:
-                        g_send[k] = (g_own[...] + s_recv[k].astype(F32)).astype(BF16)
-                        remote(g_send.at[k], g_recv.at[k], S_G, g_sem, dev(dy=-dy)).start()
+                remote(g_send.at[t], g_recv.at[t], S_G, g_sem, dev(dq=-dq, dc=dc)).start()
 
         return carry
 
@@ -255,11 +242,13 @@
 
     wait_for(pos_recv.at[pl.ds(0, 7)], pos_sem)
     positive = pos_send[OWN]
-    for j, dc, dy in line:
+    for j, dc, dq in line:
         positive += pos_recv[j]
     loss_ref[...] = (jnp.log(row_sums) - positive).reshape(BLK)
-    wait_for(g_recv.at[pl.ds(0, 3)], g_sem)
-    grad_unit = g_own[...] + s_recv[3].astype(F32) + g_recv[0].astype(F32) + g_recv[1].astype(F32) + g_recv[2].astype(F32)
+    wait_for(g_recv.at[pl.ds(0, 7)], g_sem)
+    grad_unit = g_own[...]
+    for j, dc, dq in line:
+        grad_unit += g_recv[j].astype(F32)
     inv_b = jnp.concatenate([inv[...], inv[...]], axis=1)
     unit = proj_ref[...] * inv_b
     along = jnp.sum(unit * grad_unit, axis=1, keepdims=True)
@@ -267,7 +256,7 @@
 
     for sem, ref, n in (
         (S_PLANE, u, 15), (S_ROW, rows, 7), (S_ENC, enc, 7), (S_RS, rs_send, 7), (S_RCOL, r_cols, 15), (S_RROW, r_rows, 7),
-        (S_POS, pos_send, 7), (S_G, g_send, 3), (S_SIB, s_send, 4),
+        (S_POS, pos_send, 7), (S_G, g_send, 7),
     ):
         wait_for(ref.at[pl.ds(0, n)], send_sem.at[sem])
 
@@ -301,11 +290,9 @@
             pltpu.VMEM((LINE, 1, BLK), F32),
             pltpu.VMEM((LINE, 1, BLK), F32),
             pltpu.VMEM((BLK, PROJ), F32),
-            pltpu.VMEM((RING, BLK, PROJ), BF16),
-            pltpu.VMEM((RING, BLK, PROJ), BF16),
-            pltpu.VMEM((RING, BLK, PROJ), BF16),
-            pltpu.VMEM((RING, BLK, PROJ), BF16),
-            dma((16, 2)), dma((3,)), dma, dma, dma, dma, dma, dma, dma, dma((RING,)), dma((9,)), dma, dma((2,)),
+            pltpu.VMEM((LINE, BLK, PROJ), BF16),
+            pltpu.VMEM((LINE, BLK, PROJ), BF16),
+            dma((16, 2)), dma, dma, dma, dma, dma, dma, dma, dma((8,)), dma, dma((2,)),
         ],
         compiler_params=pltpu.CompilerParams(
             collective_id=0, has_side_effects=True, vmem_limit_bytes=54850 * 1024

time: 47.1 us -> 45.9 us (0.975)
  Pallas kernels: 44 us -> 43.1 us
    pallas_call x1, Pallas kernels: 44 us -> 43.1 us  [on_device(): pl.pallas_call(kernel, out_shape=(jax.ShapeDtypeStruct((BLK,), F32), jax....]
where the time goes in v5:
time: 45.9 us; the launch traced here: 45.7 us
  Pallas kernels  43.1 us (94%)
  local copies, waits for them, and re-layouts  1.94 us (4%)
  between operations  0.65 us (1%)
    pallas_call x1, Pallas kernels, on_device(): pl.pallas_call(kernel, out_shape=(jax.ShapeDtypeStruct((BLK,), F32), jax....  43.1 us
    unnamed x4, local copies, waits for them, and re-layouts  1.94 us

profile of v5, /device:TPU:0, one launch (start us, length us, event | category | flops | bytes accessed | tf_op | source)
XLA Modules:
  0.0 45.7 jit_solution(15587028006482219198)
XLA Ops:
  0.6 0.0 copy-start
  0.6 0.7 %copy-done = s32[256]{0:T(256)S(1)} copy-done((s32[256]{0:T(256)S(1)}, s32[256]{0:T(256)}, u32[]{:S(2)}) %copy-start) | copy-done | bytes 1048
  1.3 43.1 %shard_map.41 = (f32[256]{0:T(256)S(1)}, f32[256,256]{1,0:T(8,128)S(1)}) custom-call(f32[256,256]{1,0:T(8,128)} %proj_hbm.1, s32[256]{0:T(256)S(1)} %copy-done), custom_call_target="tpu_custom_call" | custom-call | flops 8589934592 | bytes 8388608 | tf_op jit(solution)/shard_map/pallas_call | solution.py:267
  44.4 0.6 %copy.6 = f32[256]{0:T(256)} copy(f32[256]{0:T(256)S(1)} %get-tuple-element.4) | data formatting | bytes 2048
  45.0 0.7 %copy.7 = f32[256,256]{1,0:T(8,128)} copy(f32[256,256]{1,0:T(8,128)S(1)} %get-tuple-element.5) | data formatting | bytes 524288
Async XLA Ops:
  0.6 0.7 %copy-start = (s32[256]{0:T(256)S(1)}, s32[256]{0:T(256)}, u32[]{:S(2)}) copy-start(s32[256]{0:T(256)} %part_hbm.1) | copy-start | bytes 3076

commit v6 on v5

--- a/solution.py
+++ b/solution.py
@@ -25,6 +25,7 @@
 STEP = {d: s for s, d in enumerate(ORDER)}
 SLOTS = ((1, 2), (0, 2), (1, 1), (0, 1), (1, 3), (0, 3), (1, 0), (0, 0))
 OWN = 7
+CUT = 112
 TWOS = 7
 FIRST = 3
 S_PLANE, S_ROW, S_ENC, S_RS, S_RCOL, S_RROW, S_POS, S_G = range(8)
@@ -94,7 +95,7 @@
         pltpu.make_async_copy(ref, ref, sem).wait()
 
     def piece(s, half):
-        return u.at[s, pl.ds(half * 128, 128), :]
+        return u.at[s, pl.ds(half * CUT, BLK - CUT if half else CUT), :]
 
     def along(half, d):
         return (d, 0) if half == 0 else (0, d)
@@ -134,14 +135,12 @@
     c_iota = lax.broadcasted_iota(jnp.int32, (BLK, BLK), 1)
 
     def arrive(i):
-        @pl.when((i >= 1) & (i < 7))
-        def _():
-            half = lax.rem(i, 2)
-            wait_for(u.at[i, pl.ds(pl.multiple_of(half * 128, 128), 128), :], own_sem.at[i, half])
-
-        @pl.when(i >= 7)
+        @pl.when((i >= 7) | ((i > 0) & (lax.rem(i, 2) == 0)))
         def _():
             wait_half(i, 0)
+
+        @pl.when((i >= 7) | (lax.rem(i, 2) == 1))
+        def _():
             wait_half(i, 1)
 
     def compute(blocks):
@@ -169,10 +168,10 @@
     lax.fori_loop(0, TWOS, two, 0)
     lax.fori_loop(2 * TWOS, PLANE, one, 0)
 
-    for j in range(LINE):
+    for j, (dc, dq) in enumerate(SLOTS):
         rs_send[j] = transposed_sum(acc[j])
-    for j, dc, dq in line:
-        remote(rs_send.at[j], rs_recv.at[j], S_RS, rs_sem, dev(dq=-dq, dc=dc)).start()
+        if j != OWN:
+            remote(rs_send.at[j], rs_recv.at[j], S_RS, rs_sem, dev(dq=-dq, dc=dc)).start()
 
     wait_for(enc.at[pl.ds(0, 7)], enc_sem)
     v = enc[...]

time: 45.9 us -> 45 us (0.980)
  Pallas kernels: 43.1 us -> 42.2 us
    pallas_call x1, Pallas kernels: 43.1 us -> 42.2 us  [on_device(): pl.pallas_call(kernel, out_shape=(jax.ShapeDtypeStruct((BLK,), F32), jax....]
where the time goes in v6:
time: 45 us; the launch traced here: 44.8 us
  Pallas kernels  42.2 us (94%)
  local copies, waits for them, and re-layouts  1.94 us (4%)
  between operations  0.65 us (1%)
    pallas_call x1, Pallas kernels, on_device(): pl.pallas_call(kernel, out_shape=(jax.ShapeDtypeStruct((BLK,), F32), jax....  42.2 us
    unnamed x4, local copies, waits for them, and re-layouts  1.94 us

profile of v6, /device:TPU:0, one launch (start us, length us, event | category | flops | bytes accessed | tf_op | source)
XLA Modules:
  0.0 44.8 jit_solution(4945829783746266130)
XLA Ops:
  0.6 0.0 copy-start
  0.6 0.7 %copy-done = s32[256]{0:T(256)S(1)} copy-done((s32[256]{0:T(256)S(1)}, s32[256]{0:T(256)}, u32[]{:S(2)}) %copy-start) | copy-done | bytes 1048
  1.3 42.2 %shard_map.41 = (f32[256]{0:T(256)S(1)}, f32[256,256]{1,0:T(8,128)S(1)}) custom-call(f32[256,256]{1,0:T(8,128)} %proj_hbm.1, s32[256]{0:T(256)S(1)} %copy-done), custom_call_target="tpu_custom_call" | custom-call | flops 8589934592 | bytes 8388608 | tf_op jit(solution)/shard_map/pallas_call | solution.py:266
  43.5 0.6 %copy.6 = f32[256]{0:T(256)} copy(f32[256]{0:T(256)S(1)} %get-tuple-element.4) | data formatting | bytes 2048
  44.1 0.7 %copy.7 = f32[256,256]{1,0:T(8,128)} copy(f32[256,256]{1,0:T(8,128)S(1)} %get-tuple-element.5) | data formatting | bytes 524288
Async XLA Ops:
  0.6 0.7 %copy-start = (s32[256]{0:T(256)S(1)}, s32[256]{0:T(256)}, u32[]{:S(2)}) copy-start(s32[256]{0:T(256)} %part_hbm.1) | copy-start | bytes 3076

commit v7 on v6

--- a/solution.py
+++ b/solution.py
@@ -71,7 +71,7 @@
     plane = [(dx, dz) for dz in (2, 1, 3, 0) for dx in (2, 1, 3, 0) if (dx, dz) != (0, 0)]
     line = [(j, dc, dq) for j, (dc, dq) in enumerate(SLOTS) if j != OWN]
     near = [dev(dp=k) for k in (1, 2, 3)] + [dev(dz=k) for k in (1, 2, 3)] + [dev(dq=k) for k in (1, 2, 3)]
-    near += [dev(dq=k, dc=1) for k in (0, 1, 2, 3)]
+    near += [dev(dc=1)]
     barrier = pltpu.get_barrier_semaphore()
     for to in near:
         pl.semaphore_signal(barrier, inc=1, device_id=to, device_id_type=MESH)
@@ -113,10 +113,8 @@
             push(0, half, half, d)
     for half in (0, 1):
         push(0, half, half, 2)
-    for dq in (1, 3, 2, 0):
-        for dc in (0, 1):
-            if (dc, dq) != (0, 0):
-                remote(u.at[0], rows.at[SLOTS.index((dc, dq))], S_ROW, row_sem, reader(dc, dq)).start()
+    for dc, dq in ((0, 1), (0, 3), (0, 2), (1, 0)):
+        remote(u.at[0], rows.at[SLOTS.index((dc, dq))], S_ROW, row_sem, reader(dc, dq)).start()
     for half in (1, 0):
         for d in (1, 3, 2):
             push(0, half, 1 - half, d)
@@ -126,6 +124,10 @@
             wait_half(s, half)
             for f in (1, 3, 2):
                 push(s, half, 1 - half, f)
+    for d in (1, 3, 2):
+        s = STEP[(d, 0)]
+        wait_half(s, 1)
+        remote(u.at[s], rows.at[SLOTS.index((1, d))], S_ROW, row_sem, dev(dc=1)).start()
     for j, dc, dq in line:
         remote(enc.at[OWN], enc.at[j], S_ENC, enc_sem, reader(dc, dq)).start()
     wait_for(rows.at[pl.ds(0, 7)], row_sem)
@@ -139,7 +141,7 @@
         def _():
             wait_half(i, 0)
 
-        @pl.when((i >= 7) | (lax.rem(i, 2) == 1))
+        @pl.when(i >= 7)
         def _():
             wait_half(i, 1)
 
@@ -233,7 +235,7 @@
 
             @pl.when(j == t)
             def _():
-                remote(g_send.at[t], g_recv.at[t], S_G, g_sem, dev(dq=-dq, dc=dc)).start()
+                remote(g_send.at[t], g_recv.at[t], S_G, g_sem.at[t], dev(dq=-dq, dc=dc)).start()
 
         return carry
 
@@ -244,10 +246,10 @@
     for j, dc, dq in line:
         positive += pos_recv[j]
     loss_ref[...] = (jnp.log(row_sums) - positive).reshape(BLK)
-    wait_for(g_recv.at[pl.ds(0, 7)], g_sem)
+    for j in (6, 0, 1, 2, 3, 4, 5):
+        wait_for(g_recv.at[j], g_sem.at[j])
+        g_own[...] += g_recv[j].astype(F32)
     grad_unit = g_own[...]
-    for j, dc, dq in line:
-        grad_unit += g_recv[j].astype(F32)
     inv_b = jnp.concatenate([inv[...], inv[...]], axis=1)
     unit = proj_ref[...] * inv_b
     along = jnp.sum(unit * grad_unit, axis=1, keepdims=True)
@@ -291,7 +293,7 @@
             pltpu.VMEM((BLK, PROJ), F32),
             pltpu.VMEM((LINE, BLK, PROJ), BF16),
             pltpu.VMEM((LINE, BLK, PROJ), BF16),
-            dma((16, 2)), dma, dma, dma, dma, dma, dma, dma, dma((8,)), dma, dma((2,)),
+            dma((16, 2)), dma, dma, dma, dma, dma, dma, dma((7,)), dma((8,)), dma, dma((2,)),
         ],
         compiler_params=pltpu.CompilerParams(
             collective_id=0, has_side_effects=True, vmem_limit_bytes=54850 * 1024

time: 45 us -> 44.6 us (level)
  Pallas kernels: 42.2 us -> 41.4 us
    pallas_call x1, Pallas kernels: 42.2 us -> 41.4 us  [on_device(): pl.pallas_call(kernel, out_shape=(jax.ShapeDtypeStruct((BLK,), F32), jax....]
where the time goes in v7:
time: 44.6 us; the launch traced here: 44 us
  Pallas kernels  41.4 us (93%)
  local copies, waits for them, and re-layouts  1.94 us (4%)
  between operations  0.65 us (1%)
    pallas_call x1, Pallas kernels, on_device(): pl.pallas_call(kernel, out_shape=(jax.ShapeDtypeStruct((BLK,), F32), jax....  41.4 us
    unnamed x4, local copies, waits for them, and re-layouts  1.94 us

profile of v7, /device:TPU:0, one launch (start us, length us, event | category | flops | bytes accessed | tf_op | source)
XLA Modules:
  0.0 44.0 jit_solution(7933163607048228441)
XLA Ops:
  0.6 0.0 copy-start
  0.6 0.7 %copy-done = s32[256]{0:T(256)S(1)} copy-done((s32[256]{0:T(256)S(1)}, s32[256]{0:T(256)}, u32[]{:S(2)}) %copy-start) | copy-done | bytes 1048
  1.3 41.4 %shard_map.41 = (f32[256]{0:T(256)S(1)}, f32[256,256]{1,0:T(8,128)S(1)}) custom-call(f32[256,256]{1,0:T(8,128)} %proj_hbm.1, s32[256]{0:T(256)S(1)} %copy-done), custom_call_target="tpu_custom_call" | custom-call | flops 8589934592 | bytes 8388608 | tf_op jit(solution)/shard_map/pallas_call | solution.py:268
  42.8 0.6 %copy.6 = f32[256]{0:T(256)} copy(f32[256]{0:T(256)S(1)} %get-tuple-element.4) | data formatting | bytes 2048
  43.3 0.7 %copy.7 = f32[256,256]{1,0:T(8,128)} copy(f32[256,256]{1,0:T(8,128)S(1)} %get-tuple-element.5) | data formatting | bytes 524288
Async XLA Ops:
  0.6 0.7 %copy-start = (s32[256]{0:T(256)S(1)}, s32[256]{0:T(256)}, u32[]{:S(2)}) copy-start(s32[256]{0:T(256)} %part_hbm.1) | copy-start | bytes 3076

commit v8 on v7

--- a/solution.py
+++ b/solution.py
@@ -26,7 +26,6 @@
 SLOTS = ((1, 2), (0, 2), (1, 1), (0, 1), (1, 3), (0, 3), (1, 0), (0, 0))
 OWN = 7
 CUT = 112
-TWOS = 7
 FIRST = 3
 S_PLANE, S_ROW, S_ENC, S_RS, S_RCOL, S_RROW, S_POS, S_G = range(8)
 
@@ -163,12 +162,7 @@
         compute((2 * n, 2 * n + 1))
         return carry
 
-    def one(i, carry):
-        compute((i,))
-        return carry
-
-    lax.fori_loop(0, TWOS, two, 0)
-    lax.fori_loop(2 * TWOS, PLANE, one, 0)
+    lax.fori_loop(0, PLANE // 2, two, 0)
 
     for j, (dc, dq) in enumerate(SLOTS):
         rs_send[j] = transposed_sum(acc[j])

time: 44.6 us -> 44.5 us (level)
  no operation moved by 1% of the time
where the time goes in v8:
time: 44.5 us; the launch traced here: 43.9 us
  Pallas kernels  41.3 us (93%)
  local copies, waits for them, and re-layouts  1.94 us (4%)
  between operations  0.65 us (1%)
    pallas_call x1, Pallas kernels, on_device(): pl.pallas_call(kernel, out_shape=(jax.ShapeDtypeStruct((BLK,), F32), jax....  41.3 us
    unnamed x4, local copies, waits for them, and re-layouts  1.94 us

profile of v8, /device:TPU:0, one launch (start us, length us, event | category | flops | bytes accessed | tf_op | source)
XLA Modules:
  0.0 43.9 jit_solution(17746978499770781467)
XLA Ops:
  0.6 0.0 copy-start
  0.6 0.7 %copy-done = s32[256]{0:T(256)S(1)} copy-done((s32[256]{0:T(256)S(1)}, s32[256]{0:T(256)}, u32[]{:S(2)}) %copy-start) | copy-done | bytes 1048
  1.3 41.3 %shard_map.41 = (f32[256]{0:T(256)S(1)}, f32[256,256]{1,0:T(8,128)S(1)}) custom-call(f32[256,256]{1,0:T(8,128)} %proj_hbm.1, s32[256]{0:T(256)S(1)} %copy-done), custom_call_target="tpu_custom_call" | custom-call | flops 8589934592 | bytes 8388608 | tf_op jit(solution)/shard_map/pallas_call | solution.py:262
  42.6 0.6 %copy.6 = f32[256]{0:T(256)} copy(f32[256]{0:T(256)S(1)} %get-tuple-element.4) | data formatting | bytes 2048
  43.2 0.7 %copy.7 = f32[256,256]{1,0:T(8,128)} copy(f32[256,256]{1,0:T(8,128)S(1)} %get-tuple-element.5) | data formatting | bytes 524288
Async XLA Ops:
  0.6 0.7 %copy-start = (s32[256]{0:T(256)S(1)}, s32[256]{0:T(256)}, u32[]{:S(2)}) copy-start(s32[256]{0:T(256)} %part_hbm.1) | copy-start | bytes 3076

commit v9 on v8

--- a/solution.py
+++ b/solution.py
@@ -162,7 +162,8 @@
         compute((2 * n, 2 * n + 1))
         return carry
 
-    lax.fori_loop(0, PLANE // 2, two, 0)
+    compute((0, 1, 2, 3))
+    lax.fori_loop(2, PLANE // 2, two, 0)
 
     for j, (dc, dq) in enumerate(SLOTS):
         rs_send[j] = transposed_sum(acc[j])

time: 44.5 us -> 44.5 us (level)
  no operation moved by 1% of the time
where the time goes in v9:
time: 44.5 us; the launch traced here: 43.8 us
  Pallas kernels  41.2 us (93%)
  local copies, waits for them, and re-layouts  1.94 us (4%)
  between operations  0.65 us (1%)
    pallas_call x1, Pallas kernels, on_device(): pl.pallas_call(kernel, out_shape=(jax.ShapeDtypeStruct((BLK,), F32), jax....  41.2 us
    unnamed x4, local copies, waits for them, and re-layouts  1.94 us

profile of v9, /device:TPU:0, one launch (start us, length us, event | category | flops | bytes accessed | tf_op | source)
XLA Modules:
  0.0 43.8 jit_solution(6260793846414640279)
XLA Ops:
  0.6 0.0 copy-start
  0.6 0.7 %copy-done = s32[256]{0:T(256)S(1)} copy-done((s32[256]{0:T(256)S(1)}, s32[256]{0:T(256)}, u32[]{:S(2)}) %copy-start) | copy-done | bytes 1048
  1.3 41.2 %shard_map.41 = (f32[256]{0:T(256)S(1)}, f32[256,256]{1,0:T(8,128)S(1)}) custom-call(f32[256,256]{1,0:T(8,128)} %proj_hbm.1, s32[256]{0:T(256)S(1)} %copy-done), custom_call_target="tpu_custom_call" | custom-call | flops 8589934592 | bytes 8388608 | tf_op jit(solution)/shard_map/pallas_call | solution.py:263
  42.6 0.6 %copy.6 = f32[256]{0:T(256)} copy(f32[256]{0:T(256)S(1)} %get-tuple-element.4) | data formatting | bytes 2048
  43.1 0.7 %copy.7 = f32[256,256]{1,0:T(8,128)} copy(f32[256,256]{1,0:T(8,128)S(1)} %get-tuple-element.5) | data formatting | bytes 524288
Async XLA Ops:
  0.6 0.7 %copy-start = (s32[256]{0:T(256)S(1)}, s32[256]{0:T(256)}, u32[]{:S(2)}) copy-start(s32[256]{0:T(256)} %part_hbm.1) | copy-start | bytes 3076
